TPU v7x, 32 devices: a whole 2x2x4 slice. The times are simulated.
32 devices in a mesh: dp: 16 (over z, y, x), mp: 2 (over core).
Axes of the slice: x: 2, y: 2, z: 4, core: 2. Of those that a mesh axis runs over, the one named last changes fastest.
Arguments:
- inputs: float32 [32768, 512], P(('dp', 'mp')), may hold values from -6 to 6
- segment_ids: int32 [32, 1024], P('dp'), may hold values from 0 to 3, never falling along the last dimension, each value on 1 to 512 neighbouring positions
- first_gain: float32 [512], replicated, may hold values from 0.5 to 1.5
- first_shift: float32 [512], replicated, may hold values from -3 to 3
- qkv_weight: float32 [3, 512, 512], P(None, None, 'mp'), may hold values from -0.25 to 0.25
- out_weight: float32 [512, 512], P('mp'), may hold values from -1 to 1
- features: float32 [8, 256, 64], P('mp'), may hold values from -4 to 4
- second_gain: float32 [512], replicated, may hold values from 0.5 to 1.5
- second_shift: float32 [512], replicated, may hold values from -3 to 3
- in_weight: float32 [512, 2048], P(None, 'mp'), may hold values from -0.25 to 0.25
- in_bias: float32 [2048], P('mp'), may hold values from -3 to 3
- back_weight: float32 [2048, 512], P('mp'), may hold values from -0.125 to 0.125
- back_bias: float32 [512], replicated, may hold values from -3 to 3
- cotangent: float32 [32768, 512], P(('dp', 'mp')), may hold values from -6 to 6
Outputs:
- output: float32 [32768, 512], P(('dp', 'mp'))
- g_inputs: float32 [32768, 512], P(('dp', 'mp'))
- g_first_gain: float32 [512], replicated
- g_first_shift: float32 [512], replicated
- g_qkv_weight: float32 [3, 512, 512], P(None, None, 'mp')
- g_out_weight: float32 [512, 512], P('mp')
- g_second_gain: float32 [512], replicated
- g_second_shift: float32 [512], replicated
- input_weight_gradient: float32 [512, 2048], P(None, 'mp')
- g_in_bias: float32 [2048], P('mp')
- g_back_weight: float32 [2048, 512], P('mp')
- g_back_bias: float32 [512], replicated
Inputs may be any that keep to these rules, and one draw needn't show every extreme that they name: `segment_ids`: along each row the ids never fall and start at 0; each of the 4 proteins of a row has 1 to 512 tokens, one exactly 512.
All inputs are finite; a program needn't handle non-finite values.
Results may differ from a plain program's by a relative error of at most 0.0003.
Values sent between devices are 32-bit elements; how exact they have to be, the bound alone decides.
A program may use at most 320 MiB of HBM per device.

v0:
```python
import jax
import jax.numpy as jnp
from jax import lax
from jax.sharding import PartitionSpec as P

BLOCK = 512


epsilon = 1e-05
top_precision = lax.Precision.HIGHEST


def layer_norm(vector, gain, shift):
    average = jnp.mean(vector, -1, keepdims=True)
    centred = vector - average
    spread = jnp.mean(centred * centred, -1, keepdims=True)
    return centred * lax.rsqrt(spread + epsilon) * gain + shift


def feature_map(vector, features):
    scaled_values = vector * vector.shape[-1] ** (-0.25)
    project_rows = jnp.einsum("wer,esr->wes", scaled_values, features, precision=top_precision)
    return jnp.exp(
        project_rows - 0.5 * jnp.sum(scaled_values * scaled_values, -1, keepdims=True)
    ) * features.shape[1] ** (-0.5)


def block_attend(query_feats, key_feats, values_in, segment_ids):
    count_of_rows, length = segment_ids.shape
    head_count = values_in.shape[2]
    head_size = values_in.shape[3]
    feat_count = query_feats.shape[3]
    block_count = length // BLOCK

    def blockwise(array):
        return jnp.moveaxis(
            array.reshape((count_of_rows, block_count, BLOCK) + array.shape[2:]), 1, 0
        )

    causal = jnp.tril(jnp.ones((BLOCK, BLOCK), jnp.float32))

    def advance(carried, pieces):
        prefix_state, prefix_norm, last_seg = carried
        query_block, key_block, block_of_values, seg_block = pieces
        same_seg = (seg_block[:, :, None] == seg_block[:, None, :]).astype(jnp.float32) * causal
        scores = (
            jnp.einsum("rihm,rjhm->rhij", query_block, key_block, precision=top_precision)
            * same_seg[:, None]
        )
        weighted = jnp.einsum("rhij,rjhd->rihd", scores, block_of_values, precision=top_precision)
        totals = jnp.moveaxis(jnp.sum(scores, -1), 1, 2)
        continues = (seg_block == last_seg[:, None]).astype(jnp.float32)
        weighted = weighted + continues[:, :, None, None] * jnp.einsum(
            "rihm,rhmd->rihd", query_block, prefix_state, precision=top_precision
        )
        totals = totals + continues[:, :, None] * jnp.einsum(
            "rihm,rhm->rih", query_block, prefix_norm, precision=top_precision
        )
        new_last = seg_block[:, -1]
        carry_on = (new_last == last_seg).astype(jnp.float32)
        tail_mask = (seg_block == new_last[:, None]).astype(jnp.float32)
        tail_keys = key_block * tail_mask[:, :, None, None]
        prefix_state = carry_on[:, None, None, None] * prefix_state + jnp.einsum(
            "rjhm,rjhd->rhmd", tail_keys, block_of_values, precision=top_precision
        )
        prefix_norm = carry_on[:, None, None] * prefix_norm + jnp.sum(tail_keys, 1)
        return ((prefix_state, prefix_norm, new_last), weighted / totals[:, :, :, None])

    initial = (
        jnp.zeros((count_of_rows, head_count, feat_count, head_size), jnp.float32),
        jnp.zeros((count_of_rows, head_count, feat_count), jnp.float32),
        jnp.full((count_of_rows,), -1, jnp.int32),
    )
    _, mixed = lax.scan(
        advance,
        initial,
        (
            blockwise(query_feats),
            blockwise(key_feats),
            blockwise(values_in),
            blockwise(segment_ids),
        ),
    )
    return jnp.moveaxis(mixed, 0, 1).reshape(count_of_rows * length, head_count * head_size)


def attention_part(normed, qkv_weight, out_weight, features, segment_ids):
    count_of_rows, length = segment_ids.shape
    head_count, feat_count, head_size = features.shape
    project_rows = jnp.einsum("nd,cde->cne", normed, qkv_weight, precision=top_precision)
    project_rows = project_rows.reshape(3, count_of_rows * length, head_count, head_size)
    query_feats = feature_map(project_rows[0], features).reshape(
        count_of_rows, length, head_count, feat_count
    )
    key_feats = feature_map(project_rows[1], features).reshape(
        count_of_rows, length, head_count, feat_count
    )
    values_in = project_rows[2].reshape(count_of_rows, length, head_count, head_size)
    mixed = block_attend(query_feats, key_feats, values_in, segment_ids)
    return jnp.dot(mixed, out_weight, precision=top_precision)


def ffn_part(normed, in_weight, in_bias, back_weight):
    hidden = jax.nn.gelu(jnp.dot(normed, in_weight, precision=top_precision) + in_bias)
    return jnp.dot(hidden, back_weight, precision=top_precision)


def body(
    inputs,
    segment_ids,
    first_gain,
    first_shift,
    qkv_weight,
    out_weight,
    features,
    second_gain,
    second_shift,
    in_weight,
    in_bias,
    back_weight,
    back_bias,
    cotangent,
):

    def attend_local(normed, qkv_local, out_local):
        return attention_part(normed, qkv_local, out_local, features, segment_ids)

    first_normed, first_back = jax.vjp(layer_norm, inputs, first_gain, first_shift)
    first_rows = lax.all_gather(first_normed, "mp", axis=0, tiled=True)
    attn_terms, attn_back = jax.vjp(attend_local, first_rows, qkv_weight, out_weight)
    middle = inputs + lax.psum_scatter(attn_terms, "mp", scatter_dimension=0, tiled=True)
    second_normed, second_back = jax.vjp(layer_norm, middle, second_gain, second_shift)
    second_rows = lax.all_gather(second_normed, "mp", axis=0, tiled=True)
    ffn_terms, ffn_back = jax.vjp(ffn_part, second_rows, in_weight, in_bias, back_weight)
    output = middle + lax.psum_scatter(ffn_terms, "mp", scatter_dimension=0, tiled=True) + back_bias
    g_back_bias = jnp.sum(cotangent, 0)
    cot_rows = lax.all_gather(cotangent, "mp", axis=0, tiled=True)
    second_rows_gradient, input_weight_gradient, g_in_bias, g_back_weight = ffn_back(cot_rows)
    g_second_normed = lax.psum_scatter(second_rows_gradient, "mp", scatter_dimension=0, tiled=True)
    g_middle_norm, g_second_gain, g_second_shift = second_back(g_second_normed)
    middle_gradient = cotangent + g_middle_norm
    middle_rows = lax.all_gather(middle_gradient, "mp", axis=0, tiled=True)
    g_first_rows, g_qkv_weight, g_out_weight = attn_back(middle_rows)
    g_first_normed = lax.psum_scatter(g_first_rows, "mp", scatter_dimension=0, tiled=True)
    g_input_norm, g_first_gain, g_first_shift = first_back(g_first_normed)
    g_inputs = middle_gradient + g_input_norm
    g_first_gain, g_first_shift, g_second_gain, g_second_shift, g_back_bias = lax.psum(
        (g_first_gain, g_first_shift, g_second_gain, g_second_shift, g_back_bias), ("dp", "mp")
    )
    g_qkv_weight, g_out_weight, input_weight_gradient, g_in_bias, g_back_weight = lax.psum(
        (g_qkv_weight, g_out_weight, input_weight_gradient, g_in_bias, g_back_weight), "dp"
    )
    return (
        output,
        g_inputs,
        g_first_gain,
        g_first_shift,
        g_qkv_weight,
        g_out_weight,
        g_second_gain,
        g_second_shift,
        input_weight_gradient,
        g_in_bias,
        g_back_weight,
        g_back_bias,
    )


def solution(mesh):
    placed = (
        P(("dp", "mp"), None),
        P("dp", None),
        P(),
        P(),
        P(None, None, "mp"),
        P("mp", None),
        P("mp", None, None),
        P(),
        P(),
        P(None, "mp"),
        P("mp"),
        P("mp", None),
        P(),
        P(("dp", "mp"), None),
    )
    return jax.shard_map(
        body,
        mesh=mesh,
        in_specs=placed,
        out_specs=(
            P(("dp", "mp"), None),
            P(("dp", "mp"), None),
            P(),
            P(),
            P(None, None, "mp"),
            P("mp", None),
            P(),
            P(),
            P(None, "mp"),
            P("mp"),
            P("mp", None),
            P(),
        ),
        check_vma=False,
    )
```

profile of v0, /device:TPU:0, one launch (start us, length us, event | category | flops | bytes accessed | tf_op | source)
XLA Modules:
  0.0 970.5 jit_solution(14681336542917149797)
XLA Ops:
  15.9 16.4 %all-gather.5.cloned.1.call-done = f32[2048,512]{1,0:T(8,128)} async-done(((f32[1024,512]{1,0:T(8,128)}), f32[2048,512]{1,0:T(8,128)}) %all-gather.5.cloned.1.call-update) | async-done | bytes 4194320 | tf_op jit(solution)/shard_map/all_gather | solution.py:129
  32.3 13.0 %fusion.152 = f32[3,2048,256]{1,2,0:T(8,128)S(1)} fusion(f32[3,512,256]{2,1,0:T(8,128)} %param.22, f32[2048,512]{1,0:T(8,128)} %all-gather.5.cloned.1.call-done), kind=kOutput, calls=%fused_computation.188 | convolution fusion | flops 9663676416 | bytes 12058624 | tf_op jit(solution)/shard_map/jvp(nd,cde->cne)/dot_general | solution.py:90
  58.5 11.3 %fusion.147 = (f32[2048,4,256]{2,0,1:T(8,128)S(1)}, f32[4,2048,256]{2,1,0:T(8,128)}) fusion(f32[2048,4]{0,1:T(4,128)S(1)} %broadcast_multiply_fusion.1, f32[2048,4,64]{0,2,1:T(8,128)S(1)} %bitcast.477, f32[4,256,64]{1,2,0:T(8,128)S(1)} %copy-done.35), kind=kOutput, calls=%fused_computation.182 | convolution fusion | flops 1614807040 | bytes 19169280 | tf_op jit(solution)/shard_map/jvp(wer,esr->wes)/dot_general | solution.py:22
  73.6 10.6 %fusion.146 = (f32[2048,4,256]{2,0,1:T(8,128)S(1)}, f32[4,2048,256]{2,1,0:T(8,128)}) fusion(f32[2048,4]{0,1:T(4,128)S(1)} %broadcast_multiply_fusion.2, f32[2048,4,64]{0,2,1:T(8,128)S(1)} %bitcast.475, f32[4,256,64]{1,2,0:T(8,128)S(1)} %copy-done.35), kind=kOutput, calls=%fused_computation.181 | convolution fusion | flops 1614807040 | bytes 19169280 | tf_op jit(solution)/shard_map/jvp(wer,esr->wes)/dot_general | solution.py:22
  95.4 111.4 %while.68 = (s32[]{:T(128)}, f32[2,4,256,64]{2,3,1,0:T(8,128)}, f32[2,4,256]{2,1,0:T(4,128)S(1)}, s32[2]{0:T(128)S(1)}, f32[2,2,512,4,64]{2,4,3,1,0:T(8,128)}, /...) while((s32[]{:T(128)}, f32[2,4,256,64]{2,3,1,0:T(8,128)}, ...), condition=%wide.region_7.8_spmd.clone.clone, body=%wide.region_4.7_spmd.clone.clone.sunk | while | flops 9692934144 | bytes 205273776 | solution.py:74
  128.4 10.2 %multiply_reduce_fusion.10 = (f32[2,4,512]{2,1,0:T(4,128)S(1)}, f32[2,4,512,512]{2,3,1,0:T(8,128)S(1)}) fusion(f32[2,512,512]{1,2,0:T(8,128)S(1)} %compare_select_fusion.2, f32[2,2,512,4,256]{4,2,3,1,0:T(8,128)} %get-tuple-element.1475, s32[]{:T(128)S(6)} %copy.224, f32[2,2,512,4,256]{4,2,3,1,0:T(8,128)S(1)} %bitcast.457), kind=kOutput, calls=%fused_computation.89.clone.1 | convolution fusion | flops 6446641152 | bytes 18891776 | tf_op jit(solution)/shard_map/jvp()/while/body/eval_jaxpr/rihm,rjhm->rhij/dot_general | solution.py:47
  183.9 10.2 %multiply_reduce_fusion.10 = (f32[2,4,512]{2,1,0:T(4,128)S(1)}, f32[2,4,512,512]{2,3,1,0:T(8,128)S(1)}) fusion(f32[2,512,512]{1,2,0:T(8,128)S(1)} %compare_select_fusion.2, f32[2,2,512,4,256]{4,2,3,1,0:T(8,128)} %get-tuple-element.1475, s32[]{:T(128)S(6)} %copy.224, f32[2,2,512,4,256]{4,2,3,1,0:T(8,128)S(1)} %bitcast.457), kind=kOutput, calls=%fused_computation.89.clone.1 | convolution fusion | flops 6446641152 | bytes 18891776 | tf_op jit(solution)/shard_map/jvp()/while/body/eval_jaxpr/rihm,rjhm->rhij/dot_general | solution.py:47
  215.4 9.9 %fusion.203 = f32[2048,512]{1,0:T(8,128)} fusion(f32[2048,256]{0,1:T(8,128)} %reshape.370, f32[256,512]{1,0:T(8,128)S(1)} %copy-done.38), kind=kOutput, calls=%fused_computation.250 | convolution fusion | flops 3221225472 | bytes 6815744 | tf_op jit(solution)/shard_map/jvp()/dot_general | solution.py:100
  225.4 13.3 %reduce-scatter.5.cloned.1.call-done = f32[1024,512]{1,0:T(8,128)} async-done(((f32[2048,512]{1,0:T(8,128)}), f32[1024,512]{1,0:T(8,128)}) %reduce-scatter.5.cloned.1.call-update) | async-done | bytes 2097168 | tf_op jit(solution)/shard_map/reduce_scatter | solution.py:131
  244.9 14.5 %all-gather.7.cloned.1.call-done = f32[2048,512]{1,0:T(8,128)} async-done(((f32[1024,512]{1,0:T(8,128)}), f32[2048,512]{1,0:T(8,128)}) %all-gather.7.cloned.1.call-update) | async-done | bytes 4194320 | tf_op jit(solution)/shard_map/all_gather | solution.py:133
  259.4 18.0 %fusion.204 = f32[2048,1024]{1,0:T(8,128)} fusion(f32[2048,512]{1,0:T(8,128)} %all-gather.7.cloned.1.call-done, f32[512,1024]{1,0:T(8,128)} %param.27), kind=kOutput, calls=%fused_computation.251 | convolution fusion | flops 12884901888 | bytes 14680064 | tf_op jit(solution)/shard_map/jvp()/dot_general | solution.py:104
  277.4 23.2 %fusion.202 = (f32[1024]{0:T(1024)}, f32[2048,1024]{1,0:T(8,128)S(1)}) fusion(f32[2048,1024]{1,0:T(8,128)} %fusion.204, f32[1024]{0:T(1024)S(1)} %copy-done.68, f32[2048,512]{1,0:T(8,128)} %all-gather.9.cloned.1.call-done, f32[1024,512]{1,0:T(8,128)S(1)} %copy-done), kind=kOutput, calls=%fused_computation.249 | convolution fusion | flops 12928941056 | bytes 23076864 | tf_op jit(solution)/shard_map/transpose(jvp())/dot_general | solution.py:105
  303.8 15.0 %fusion.205 = f32[2048,512]{1,0:T(8,128)} fusion(f32[2048,1024]{1,0:T(8,128)S(1)} %get-tuple-element.1091, f32[512,1024]{1,0:T(8,128)S(1)} %copy-done.37), kind=kOutput, calls=%fused_computation.252 | convolution fusion | flops 12884901888 | bytes 14680064 | tf_op jit(solution)/shard_map/transpose(jvp())/dot_general | solution.py:104
  318.8 19.5 %fusion.156 = f32[2048,512]{1,0:T(8,128)} fusion(f32[1024,512]{1,0:T(8,128)S(1)} %copy-done, f32[2048,1024]{1,0:T(8,128)} %fusion.204, f32[1024]{0:T(1024)S(1)} %copy-done.68), kind=kOutput, calls=%fused_computation.193 | convolution fusion | flops 12903776256 | bytes 14684160 | tf_op jit(solution)/shard_map/jvp()/dot_general | solution.py:105
  342.9 8.8 reduce-scatter.7.cloned.1.call-done
  357.8 18.7 %fusion.208 = f32[512,1024]{1,0:T(8,128)} fusion(f32[2048,512]{1,0:T(8,128)} %all-gather.7.cloned.1.call-done, f32[2048,1024]{1,0:T(8,128)} %copy-done.70), kind=kOutput, calls=%fused_computation.255 | convolution fusion | flops 12884901888 | bytes 14680064 | tf_op jit(solution)/shard_map/transpose(jvp())/dot_general | solution.py:104
  376.6 19.3 %fusion.155 = f32[1024,512]{1,0:T(8,128)} fusion(f32[2048,512]{1,0:T(8,128)S(1)} %copy-done.67, f32[2048,1024]{1,0:T(8,128)} %fusion.204, f32[1024]{0:T(1024)S(1)} %copy-done.68), kind=kOutput, calls=%fused_computation.192 | convolution fusion | flops 12903776256 | bytes 14684160 | tf_op jit(solution)/shard_map/transpose(jvp())/dot_general | solution.py:105
  414.2 185.6 %while.67 = (s32[]{:T(128)}, f32[2,4,256,64]{2,3,1,0:T(8,128)S(1)}, f32[2,4,256]{2,1,0:T(4,128)S(1)}, f32[2,2,512,4,256]{4,2,3,1,0:T(8,128)}, f32[2,2,512,4,256]...) while((s32[]{:T(128)}, f32[2,4,256,64]{2,3,1,0:T(8,128)S(1)}, ...), condition=%wide.region_17.18_spmd.clone, body=%wide.region_15.17_spmd.clone.sunk | while | flops 19357915136 | bytes 230941456 | solution.py:74
  455.4 10.6 %fusion.302 = f32[2,2,512,4,64]{2,4,3,1,0:T(8,128)S(1)} fusion(f32[2,2,512,4,64]{2,4,3,1,0:T(8,128)S(1)} %copy-done.29, s32[]{:T(128)S(6)} %sub.100, f32[2,512,4,64]{1,3,2,0:T(8,128)S(1)} %fusion.301, f32[2,2,4,512,512]{3,4,2,1,0:T(8,128)} %get-tuple-element.1552, f32[1,2,512,4,64]{2,0,1,4,3:T(1,128)S(1)} %constant_dynamic-slice_fusion.8, ...), kind=kOutput, calls=%fused_computation.31.clone.1 | convolution fusion | flops 1611137024 | bytes 11551744 | tf_op jit(solution)/shard_map/transpose(jvp())/while/body/eval_jaxpr/rhij,rjhd->rihd/dot_general | solution.py:50
  474.1 15.6 %fusion.300 = f32[2,4,512,256]{3,2,1,0:T(8,128)} fusion(f32[2,4,512,512]{3,2,1,0:T(8,128)S(1)} %fusion.298, f32[2,512,512]{2,1,0:T(8,128)S(1)} %dynamic-slice_bitcast_fusion.8, f32[2,4,512]{2,1,0:T(4,128)S(1)} %negate_bitcast_fusion.2, f32[2,2,512,4,256]{4,2,3,1,0:T(8,128)S(1)} %bitcast.459, s32[]{:T(128)S(6)} %sub.100), kind=kOutput, calls=%fused_computation.5.clone.1 | convolution fusion | flops 6446645248 | bytes 18890756 | tf_op jit(solution)/shard_map/transpose(jvp())/while/body/eval_jaxpr/rihm,rjhm->rhij/dot_general | solution.py:47
  489.7 9.9 %fusion.299 = f32[2,4,512,256]{3,2,1,0:T(8,128)S(1)} fusion(f32[2,4,512,512]{3,2,1,0:T(8,128)S(1)} %fusion.298, f32[2,2,512,4,256]{4,2,3,1,0:T(8,128)} %get-tuple-element.1549, s32[]{:T(128)S(6)} %sub.100, f32[2,512,512]{2,1,0:T(8,128)S(1)} %dynamic-slice_bitcast_fusion.8, f32[2,4,512]{2,1,0:T(4,128)S(1)} %negate_bitcast_fusion.2), kind=kOutput, calls=%fused_computation.6.clone.1 | convolution fusion | flops 6446645248 | bytes 18890756 | tf_op jit(solution)/shard_map/transpose(jvp())/while/body/eval_jaxpr/rihm,rjhm->rhij/dot_general | solution.py:47
  532.9 10.6 %fusion.302 = f32[2,2,512,4,64]{2,4,3,1,0:T(8,128)S(1)} fusion(f32[2,2,512,4,64]{2,4,3,1,0:T(8,128)S(1)} %copy-done.29, s32[]{:T(128)S(6)} %sub.100, f32[2,512,4,64]{1,3,2,0:T(8,128)S(1)} %fusion.301, f32[2,2,4,512,512]{3,4,2,1,0:T(8,128)} %get-tuple-element.1552, f32[1,2,512,4,64]{2,0,1,4,3:T(1,128)S(1)} %constant_dynamic-slice_fusion.8, ...), kind=kOutput, calls=%fused_computation.31.clone.1 | convolution fusion | flops 1611137024 | bytes 11551744 | tf_op jit(solution)/shard_map/transpose(jvp())/while/body/eval_jaxpr/rhij,rjhd->rihd/dot_general | solution.py:50
  551.7 15.6 %fusion.300 = f32[2,4,512,256]{3,2,1,0:T(8,128)} fusion(f32[2,4,512,512]{3,2,1,0:T(8,128)S(1)} %fusion.298, f32[2,512,512]{2,1,0:T(8,128)S(1)} %dynamic-slice_bitcast_fusion.8, f32[2,4,512]{2,1,0:T(4,128)S(1)} %negate_bitcast_fusion.2, f32[2,2,512,4,256]{4,2,3,1,0:T(8,128)S(1)} %bitcast.459, s32[]{:T(128)S(6)} %sub.100), kind=kOutput, calls=%fused_computation.5.clone.1 | convolution fusion | flops 6446645248 | bytes 18890756 | tf_op jit(solution)/shard_map/transpose(jvp())/while/body/eval_jaxpr/rihm,rjhm->rhij/dot_general | solution.py:47
  567.2 9.9 %fusion.299 = f32[2,4,512,256]{3,2,1,0:T(8,128)S(1)} fusion(f32[2,4,512,512]{3,2,1,0:T(8,128)S(1)} %fusion.298, f32[2,2,512,4,256]{4,2,3,1,0:T(8,128)} %get-tuple-element.1549, s32[]{:T(128)S(6)} %sub.100, f32[2,512,512]{2,1,0:T(8,128)S(1)} %dynamic-slice_bitcast_fusion.8, f32[2,4,512]{2,1,0:T(4,128)S(1)} %negate_bitcast_fusion.2), kind=kOutput, calls=%fused_computation.6.clone.1 | convolution fusion | flops 6446645248 | bytes 18890756 | tf_op jit(solution)/shard_map/transpose(jvp())/while/body/eval_jaxpr/rihm,rjhm->rhij/dot_general | solution.py:47
  630.3 13.5 %fusion.197 = (f32[2048,4]{0,1:T(4,128)S(1)}, f32[2048,4,256]{2,0,1:T(8,128)}, f32[2048,4]{0,1:T(4,128)S(1)}, f32[2048,4,256]{2,0,1:T(8,128)}) fusion(f32[2048,4]{0,1:T(4,128)S(1)} %copy-done.43, f32[4,2048,256]{2,1,0:T(8,128)S(1)} %bitcast.469, f32[2,2,512,4,256]{4,2,1,0,3:T(8,128)} %copy.118, f32[2048,4]{0,1:T(4,128)S(1)} %copy-done.45, ...), kind=kLoop, calls=%fused_computation.244 | loop fusion | flops 12566528 | bytes 50462720 | tf_op jit(solution)/shard_map/transpose(jvp())/reduce_sum | solution.py:24
  643.9 10.9 %fusion.178 = f32[1,2048,4,64]{1,3,2,0:T(8,128)S(1)} fusion(f32[4,256,64]{1,2,0:T(8,128)S(1)} %copy-done.36, f32[2048,4,256]{2,0,1:T(8,128)} %get-tuple-element.1058, f32[2048,4,64]{0,2,1:T(8,128)S(1)} %bitcast.481, f32[2048,4]{0,1:T(4,128)S(1)} %negate_multiply_fusion.1), kind=kOutput, calls=%fused_computation.201 | convolution fusion | flops 1612185600 | bytes 12877824 | tf_op jit(solution)/shard_map/transpose(jvp(wer,esr->wes))/dot_general | solution.py:22
  670.4 11.6 %fusion.181 = f32[3,512,256]{1,2,0:T(8,128)} fusion(f32[3,256,2048]{2,1,0:T(8,128)S(1)} %bitcast.472, f32[2048,512]{1,0:T(8,128)S(1)} %copy-done.25), kind=kOutput, calls=%fused_computation.220 | convolution fusion | flops 9663676416 | bytes 12058624 | tf_op jit(solution)/shard_map/transpose(jvp(nd,cde->cne))/dot_general | solution.py:90
  683.4 23.2 %convolution_bitcast_fusion = f32[2048,512]{1,0:T(8,128)} fusion(f32[3,256,2048]{2,1,0:T(8,128)} %bitcast.473, f32[3,512,256]{2,1,0:T(8,128)S(1)} %copy-done.39), kind=kOutput, calls=%fused_computation.189 | convolution fusion | flops 9663676416 | bytes 12058624 | tf_op jit(solution)/shard_map/transpose(jvp(nd,cde->cne))/dot_general | solution.py:90
  707.3 44.5 %psum.77 = f32[1024]{0:T(1024)} all-reduce(f32[1024]{0:T(1024)S(1)} %copy-done.63), channel_id=1, replica_groups=mesh['dp'=16,'mp'=2] {'dp'}, use_global_device_ids=true, to_apply=%region_35.36 | all-reduce | flops 1024 | bytes 8192 | tf_op jit(solution)/shard_map/psum | solution.py:150
  751.8 144.9 %all-reduce.7.cloned.1.call-done = (f32[3,512,256]{1,2,0:T(8,128)}, f32[256,512]{1,0:T(8,128)}, f32[512,1024]{1,0:T(8,128)}, f32[1024,512]{1,0:T(8,128)}) async-done(((f32[3,512,256]{1,2,0:T(8,128)}, f32[256,512]{1,0:T(8,128)}, f32[512,1024]{1,0:T(8,128)}, f32[1024,512]{1,0:T(8,128)}), (f32[3,512,256]{1,2,0:T(8,128)}, f32[256,512]{1,0:T(8,128)}, f32[512,1024]{1,0:T(8,128)}, ...) | async-done | bytes 6291472 | tf_op jit(solution)/shard_map/psum | solution.py:150
  899.7 10.4 %reduce-scatter.11.cloned.1.call-done = f32[1024,512]{1,0:T(8,128)} async-done(((f32[2048,512]{1,0:T(8,128)}), f32[1024,512]{1,0:T(8,128)}) %reduce-scatter.11.cloned.1.call-update) | async-done | bytes 2097168 | tf_op jit(solution)/shard_map/reduce_scatter | solution.py:144
  915.9 40.8 %all-reduce.3 = (f32[512]{0:T(512)}, f32[512]{0:T(512)}, f32[512]{0:T(512)}, f32[512]{0:T(512)}, f32[512]{0:T(512)}) all-reduce(f32[512]{0:T(512)S(1)} %get-tuple-element.944, f32[512]{0:T(512)S(1)} %get-tuple-element.947, f32[512]{0:T(512)S(1)} %copy-done.61, f32[512]{0:T(512)S(1)} %copy-done.62, ...), channel_id=1, replica_groups=mesh['dp'=16,'mp'=2] {'dp','mp'}, use_global_device_ids=true, to_apply=%region_24.25 | all-reduce | flops 2560 | bytes 20480 | tf_op jit(solution)/shard_map/psum | solution.py:147
  (395 shorter events, 320.6 us)
Async XLA Ops:
  7.2 270.2 %copy-start = (f32[1024,512]{1,0:T(8,128)S(1)}, f32[1024,512]{1,0:T(8,128)}, u32[]{:S(2)}) copy-start(f32[1024,512]{1,0:T(8,128)} %param.29) | copy-start | bytes 6291460
  7.2 25.0 %all-gather.5.cloned.1.call-start = ((), (), s32[]{:S(2)}) async-start(), calls=%async_computation.4 | async-start | bytes 6291456 | tf_op jit(solution)/shard_map/all_gather | solution.py:129
  15.7 222.9 %reduce-scatter.5.cloned.1.call-start = ((), (), s32[]{:S(2)}) async-start(), calls=%async_computation.5 | async-start | bytes 6291456 | tf_op jit(solution)/shard_map/reduce_scatter | solution.py:131
  49.9 23.6 %copy-start.42 = (f32[2048,4]{0,1:T(4,128)}, f32[2048,4]{0,1:T(4,128)S(1)}, u32[]{:S(2)}) copy-start(f32[2048,4]{0,1:T(4,128)S(1)} %broadcast_multiply_fusion.2) | copy-start | bytes 98308
  108.7 17.3 %slice-start.4 = ((s8[8388608]{0:T(1024)(128)(4,1)}), s8[4194304]{0:T(1024)(128)(4,1)S(1)}, s32[]{:S(2)}) async-start(s8[8388608]{0:T(1024)(128)(4,1)} %bitcast.461), calls=%async_computation.17 | async-start | bytes 8388608 | tf_op jit(solution)/shard_map/jvp()/while
  164.1 17.5 %slice-start.4 = ((s8[8388608]{0:T(1024)(128)(4,1)}), s8[4194304]{0:T(1024)(128)(4,1)S(1)}, s32[]{:S(2)}) async-start(s8[8388608]{0:T(1024)(128)(4,1)} %bitcast.461), calls=%async_computation.17 | async-start | bytes 8388608 | tf_op jit(solution)/shard_map/jvp()/while
  165.7 13.5 %copy-start.13 = (f32[2,2,1,512,512]{4,3,2,1,0:T(8,128)S(1)}, f32[2,2,1,512,512]{4,3,2,1,0:T(8,128)}, u32[]{:S(2)}) copy-start(f32[2,2,1,512,512]{4,3,2,1,0:T(8,128)} %get-tuple-element.1437) | copy-start | bytes 12582916 | tf_op jit(solution)/shard_map/jvp()/while
  225.3 17.2 %copy-start.57 = (f32[512]{0:T(512)S(1)}, f32[512]{0:T(512)}, u32[]{:S(2)}) copy-start(f32[512]{0:T(512)} %param.25) | copy-start | bytes 6148
  225.3 17.2 %copy-start.65 = (f32[512]{0:T(512)S(1)}, f32[512]{0:T(512)}, u32[]{:S(2)}) copy-start(f32[512]{0:T(512)} %param.26) | copy-start | bytes 6148
  225.4 34.0 %all-gather.7.cloned.1.call-start = ((), (), s32[]{:S(2)}) async-start(), calls=%async_computation.6 | async-start | bytes 6291456 | tf_op jit(solution)/shard_map/all_gather | solution.py:133
  244.2 33.1 %all-gather.9.cloned.1.call-start = ((), (), s32[]{:S(2)}) async-start(), calls=%async_computation.8 | async-start | bytes 6291456 | tf_op jit(solution)/shard_map/all_gather | solution.py:137
  244.8 32.5 %copy-start.68 = (f32[1024]{0:T(1024)S(1)}, f32[1024]{0:T(1024)}, u32[]{:S(2)}) copy-start(f32[1024]{0:T(1024)} %param.28) | copy-start | bytes 12292
  244.8 93.6 %reduce-scatter.9.cloned.1.call-start = ((), (), s32[]{:S(2)}) async-start(), calls=%async_computation.9 | async-start | bytes 6291456 | tf_op jit(solution)/shard_map/reduce_scatter | solution.py:139
  277.3 26.4 %copy-start.37 = (f32[512,1024]{1,0:T(8,128)S(1)}, f32[512,1024]{1,0:T(8,128)}, u32[]{:S(2)}) copy-start(f32[512,1024]{1,0:T(8,128)} %param.27) | copy-start | bytes 6291460
  318.8 33.0 %reduce-scatter.7.cloned.1.call-start = ((), (), s32[]{:S(2)}) async-start(), calls=%async_computation.7 | async-start | bytes 6291456 | tf_op jit(solution)/shard_map/reduce_scatter | solution.py:135
  338.4 13.4 %copy-start.66 = (f32[512]{0:T(512)S(1)}, f32[512]{0:T(512)}, u32[]{:S(2)}) copy-start(f32[512]{0:T(512)} %param.30) | copy-start | bytes 6148
  338.4 57.5 %all-gather.11.cloned.1.call-start = ((), (), s32[]{:S(2)}) async-start(), calls=%async_computation.10 | async-start | bytes 6291456 | tf_op jit(solution)/shard_map/all_gather | solution.py:142
  357.8 538.9 %all-reduce.7.cloned.1.call-start = ((), (), s32[]{:S(2)}) async-start(), calls=%async_computation.12 | async-start | bytes 12582912 | tf_op jit(solution)/shard_map/psum | solution.py:150
  357.8 18.7 %copy-start.67 = (f32[2048,512]{1,0:T(8,128)S(1)}, f32[2048,512]{1,0:T(8,128)}, u32[]{:S(2)}) copy-start(f32[2048,512]{1,0:T(8,128)} %all-gather.9.cloned.1.call-done) | copy-start | bytes 12582916
  455.4 18.7 %slice-start.2 = ((s8[8388608]{0:T(1024)(128)(4,1)}), s8[4194304]{0:T(1024)(128)(4,1)S(1)}, s32[]{:S(2)}) async-start(s8[8388608]{0:T(1024)(128)(4,1)} %bitcast.458), calls=%async_computation.15 | async-start | bytes 8388608 | tf_op jit(solution)/shard_map/transpose(jvp())/while
  532.9 18.7 %slice-start.2 = ((s8[8388608]{0:T(1024)(128)(4,1)}), s8[4194304]{0:T(1024)(128)(4,1)S(1)}, s32[]{:S(2)}) async-start(s8[8388608]{0:T(1024)(128)(4,1)} %bitcast.458), calls=%async_computation.15 | async-start | bytes 8388608 | tf_op jit(solution)/shard_map/transpose(jvp())/while
  614.7 15.5 %slice-start.6 = ((s8[8388608]{0:T(1024)(128)(4,1)}), s8[4194304]{0:T(1024)(128)(4,1)S(1)}, s32[]{:S(2)}) async-start(s8[8388608]{0:T(1024)(128)(4,1)} %bitcast.466), calls=%async_computation.19 | async-start | bytes 8388608
  614.7 15.5 %slice-start.8 = ((s8[8388608]{0:T(1024)(128)(4,1)}), s8[4194304]{0:T(1024)(128)(4,1)S(1)}, s32[]{:S(2)}) async-start(s8[8388608]{0:T(1024)(128)(4,1)} %bitcast.468), calls=%async_computation.21 | async-start | bytes 8388608
  630.3 13.6 %copy-start.34 = (f32[1,2048,256]{1,2,0:T(8,128)S(1)}, f32[1,2048,256]{1,2,0:T(8,128)}, u32[]{:S(2)}) copy-start(f32[1,2048,256]{1,2,0:T(8,128)} %get-tuple-element.1078) | copy-start | bytes 6291460
  630.3 13.6 %copy-start.36 = (f32[4,256,64]{1,2,0:T(8,128)S(1)}, f32[4,256,64]{1,2,0:T(8,128)}, u32[]{:S(2)}) copy-start(f32[4,256,64]{1,2,0:T(8,128)} %param.24) | copy-start | bytes 786436
  682.0 228.1 %reduce-scatter.11.cloned.1.call-start = ((), (), s32[]{:S(2)}) async-start(), calls=%async_computation.11 | async-start | bytes 6291456 | tf_op jit(solution)/shard_map/reduce_scatter | solution.py:144
  706.6 203.6 %copy-start.9 = (f32[1024,512]{1,0:T(8,128)S(1)}, f32[1024,512]{1,0:T(8,128)}, u32[]{:S(2)}) copy-start(f32[1024,512]{1,0:T(8,128)} %param.18) | copy-start | bytes 6291460
  706.6 203.6 %copy-start.50 = (f32[1024]{0:T(1024)S(1)}, f32[1024]{0:T(1024)}, u32[]{:S(2)}) copy-start(f32[1024]{0:T(1024)} %copy-done.49) | copy-start | bytes 12292
  706.6 203.6 %copy-start.52 = (f32[1024]{0:T(1024)S(1)}, f32[1024]{0:T(1024)}, u32[]{:S(2)}) copy-start(f32[1024]{0:T(1024)} %copy-done.51) | copy-start | bytes 12292
  706.6 203.6 %copy-start.59 = (f32[512]{0:T(512)S(1)}, f32[512]{0:T(512)}, u32[]{:S(2)}) copy-start(f32[512]{0:T(512)} %param.20) | copy-start | bytes 6148
  706.6 206.1 %copy-start.56 = (f32[1024]{0:T(1024)S(1)}, f32[1024]{0:T(1024)}, u32[]{:S(2)}) copy-start(f32[1024]{0:T(1024)} %copy-done.55) | copy-start | bytes 12292
  913.7 43.0 %copy-start.40 = (f32[256,512]{1,0:T(8,128)S(1)}, f32[256,512]{1,0:T(8,128)}, u32[]{:S(2)}) copy-start(f32[256,512]{1,0:T(8,128)} %get-tuple-element.1560) | copy-start | bytes 1572868
  (83 other events, 485.6 us)
Sparse Core Ops, SparseCore 0:
  15.9 16.3 all-gather.4
  225.4 13.1 reduce-scatter.4
  244.4 14.9 all-gather.6
  260.8 14.8 all-gather.8
  318.9 13.1 reduce-scatter.8
  338.5 13.2 reduce-scatter.6
  357.9 14.9 all-gather.10
  682.2 214.4 all-reduce.6
  899.1 11.0 reduce-scatter.10
where the time goes:
time: 979 us; the launch traced here: 971 us
  matrix products  426 us (44%)
  waiting for transfers between devices  209 us (21%)
  local copies, waits for them, and re-layouts  115 us (12%)
  other arithmetic  88.7 us (9%)
  blocking collectives  85.3 us (9%)
  loops' own time  31.7 us (3%)
  between operations  14.8 us (2%)
    psum x1, waiting for transfers between devices, body(): lax.psum((g_qkv_weight, g_out_weight, input_weight_gradient, g_in_bias, g...  145 us
    dot_general x6, matrix products, advance(): jnp.einsum('rihm,rjhm->rhij', query_block, key_block, precision=top_preci...  71.2 us
    dot_general x3, matrix products, ffn_part(): return jnp.dot(hidden, back_weight, precision=top_precision)  62.1 us
    dot_general x3, matrix products, ffn_part(): jnp.dot(normed, in_weight, precision=top_precision) + in_bias  51.6 us
    dot_general x3, matrix products, attention_part(): jnp.einsum('nd,cde->cne', normed, qkv_weight, precision=top_precision)  47.7 us
    dot_general x6, matrix products, advance(): jnp.einsum('rhij,rjhd->rihd', scores, block_of_values, precision=top_prec...  47.5 us
    psum x1, blocking collectives, body(): lax.psum((g_qkv_weight, g_out_weight, input_weight_gradient, g_in_bias, g...  44.5 us
    dot_general x4, matrix products, feature_map(): jnp.einsum('wer,esr->wes', scaled_values, features, precision=top_precision)  41 us
  transfers between devices with their start and end apart: 9, of which 6 were waited for; matrix products, arithmetic and copies ran while one was open for 11% of the time, Pallas kernels for 0%

commit v1 on v0

v1 whole, which is shorter than its diff:
```python
import functools
import math

import jax
import jax.numpy as jnp
from jax import lax
from jax.experimental import pallas as pl
from jax.experimental.pallas import tpu as pltpu
from jax.sharding import PartitionSpec as P

f32 = jnp.float32
bf16 = jnp.bfloat16
EPS = 1e-05
C = 256
BH = 256
VMEM_LIMIT = 60 * 1024 * 1024
MESH = pl.DeviceIdType.MESH
NN = (((1,), (0,)), ((), ()))
NT = (((1,), (1,)), ((), ()))
TN = (((0,), (0,)), ((), ()))


def split(x):
    hi = x.astype(bf16)
    return hi, (x - hi.astype(f32)).astype(bf16)


def dot(a, b, dims=NN):
    return lax.dot_general(a, b, dims, preferred_element_type=f32)


def dot3(a, b, dims=NN):
    left, right = dims[0][0][0], dims[0][1][0]
    return dot(jnp.concatenate([a[0], a[0], a[1]], left), jnp.concatenate([b[0], b[1], b[0]], right), dims)


def stats(v):
    mean = jnp.mean(v, -1, keepdims=True)
    centred = v - mean
    rs = lax.rsqrt(jnp.mean(centred * centred, -1, keepdims=True) + EPS)
    return centred * rs, rs


def lanes(n):
    return lax.broadcasted_iota(jnp.int32, (n, 128), 1)


def half_split(x):
    hi = x.astype(bf16).astype(f32)
    return hi, x - hi


def swap_halves(x):
    return pltpu.roll(x, 64, 1)


def pack(first, second):
    return jnp.concatenate([first.astype(bf16), second.astype(bf16)], 1)


def left_pack(x, extra, lane):
    hi, lo = half_split(x)
    hi_turned = swap_halves(hi)
    return (
        pack(jnp.where(lane < 64, hi, swap_halves(lo)), jnp.where(lane < 64, hi, extra)),
        pack(jnp.where(lane < 64, hi_turned, lo), jnp.where(lane < 64, hi_turned, extra)),
    )


def right_pack(x, extras, lane):
    hi, lo = half_split(x)
    hi_turned = swap_halves(hi)

    def second(low, e):
        e_hi, e_lo = half_split(e)
        return jnp.where(lane < 64, low, jnp.where(lane < 66, e_hi, jnp.where(lane == 66, e_lo, 0.0)))

    return (
        pack(jnp.where(lane < 64, hi, hi_turned), second(lo, extras[0])),
        pack(jnp.where(lane < 64, hi_turned, hi), second(swap_halves(lo), extras[1])),
    )


def stack_rows(x, order):
    halves = half_split(x)
    row = lax.broadcasted_iota(jnp.int32, (16, x.shape[1]), 0)
    last = jnp.zeros((16, x.shape[1]), f32)
    for i, which in enumerate(order):
        last = jnp.where(row == i, halves[which][64:65], last)
    blocks = [halves[which][:64] for which in order] + [last, jnp.zeros((48, x.shape[1]), f32)]
    return jnp.concatenate(blocks, 0).astype(bf16)


def wide(x):
    hi, lo = split(x)
    return jnp.concatenate([hi, lo], 1)


def fold(x):
    return x[:, :128] + x[:, 128:]


def with_row(x, row, at):
    place = lax.broadcasted_iota(jnp.int32, (16, x.shape[1]), 0)
    return jnp.concatenate([x, jnp.where(place == at, row, 0.0)], 0)


def make_masks(masks, segc, segr, segs):
    ids = segs[pl.ds(lax.axis_index("mp"), 1), :].astype(f32)
    segr[...] = ids
    for c in range(segc.shape[0] // C):
        segc[c * C : (c + 1) * C, :] = jnp.broadcast_to(ids[:, c * C : (c + 1) * C], (128, C)).T
    row = lax.broadcasted_iota(jnp.int32, (C, C), 0)
    col = lax.broadcasted_iota(jnp.int32, (C, C), 1)
    for c in range(segc.shape[0] // C):
        same = segc[c * C : (c + 1) * C, 0:1] == segr[:, c * C : (c + 1) * C]
        masks[c] = jnp.where(same & (row >= col), 1.0, 0.0)


def seg_flags(segc, segr, c):
    rows, row = segc[c * C : (c + 1) * C, 0:1], segr[:, c * C : (c + 1) * C]
    last = segc[(c + 1) * C - 1 : (c + 1) * C, 0:1]
    tail = ((rows == last).astype(f32), (row == last).astype(f32))
    if c == 0:
        return None, tail, None
    before = segc[c * C - 1 : c * C, 0:1]
    return ((rows == before).astype(f32), (row == before).astype(f32)), tail, (last == before).astype(f32)


def attn_fwd(
    x, gain, shift, segs, w, features,
    sq, sk, vv, qfh, qfl, kfh, kfl, ah, al, sp, mixed, invt, fback, wh, wl,
    qs, ks, vs, n1h, n1l, masks, segc, segr, wv, fv, load, mp_ss, mp_rs,
):
    step = pl.program_id(0)
    side = step // 2
    pair = step % 2
    tokens = x.shape[0]
    chunks = tokens // C
    scale = 64.0 ** -0.25
    other = {"mp": 1 - lax.axis_index("mp")}
    swaps = [
        pltpu.make_async_remote_copy(
            src_ref=ref.at[0], dst_ref=ref.at[1], send_sem=mp_ss.at[i], recv_sem=mp_rs.at[i], device_id=other, device_id_type=MESH
        )
        for i, ref in enumerate((wv, fv))
    ]

    def project(which):
        ws = [split(wv[which, i]) for i in range(3)]
        for c in range(chunks):
            rows = pl.ds(c * C, C)
            n1 = (n1h[rows, :], n1l[rows, :])
            qs[rows, :] = dot3(n1, ws[0]) * scale
            ks[rows, :] = dot3(n1, ws[1]) * scale
            vs[rows, :] = dot3(n1, ws[2])

    @pl.when(step == 0)
    def _():
        own = [pltpu.make_async_copy(src, dst.at[0], load.at[i]) for i, (src, dst) in enumerate(((w, wv), (features, fv)))]
        for copy in own:
            copy.start()
        barrier = pltpu.get_barrier_semaphore()
        pl.semaphore_signal(barrier, inc=1, device_id=other, device_id_type=MESH)
        for c in range(chunks):
            rows = pl.ds(c * C, C)
            n, _ = stats(x[rows, :])
            n1h[rows, :], n1l[rows, :] = split(n * gain[...] + shift[...])
        make_masks(masks, segc, segr, segs)
        for copy in own:
            copy.wait()
        pl.semaphore_wait(barrier, 1)
        for copy in swaps:
            copy.start()
        project(0)

    @pl.when(step == 2)
    def _():
        for copy in swaps:
            copy.wait()
        project(1)

    at = pl.ds(pl.multiple_of(pair * 128, 128), 128)
    for i in range(3):
        wh[i], wl[i] = split(wv[side, i, :, at])
    lane = lanes(C)
    m = features.shape[2]
    ones = jnp.where(lane == 64, 1.0, 0.0)
    fright = []
    for h in range(2):
        fhi, flo = half_split(fv[side, pair * 2 + h])
        gap = jnp.zeros_like(fhi)
        fright.append(jnp.concatenate([fhi, fhi, flo, gap], 0).astype(bf16))
        fback[h] = jnp.concatenate([gap, fhi, gap, flo] if h else [fhi, gap, flo, gap], 0).astype(bf16)

    def feats(s):
        squares = s * s
        left = left_pack(s, 0.0, lane)
        out = []
        for h in range(2):
            half = 0.5 * jnp.sum(jnp.where(lane // 64 == h, squares, 0.0), -1, keepdims=True) + 0.5 * math.log(m)
            out.append(split(jnp.exp(dot(left[h], fright[h]) - half)))
        return out

    state = [None, None]
    for c in range(chunks):
        rows = pl.ds(c * C, C)
        q, k, v = qs[rows, at], ks[rows, at], vs[rows, at]
        sq[rows, :] = q
        sk[rows, :] = k
        vv[rows, :] = v
        qf = feats(q)
        kf = feats(k)
        cont, tail, carry = seg_flags(segc, segr, c)
        vt = v.T
        nums = []
        for h in range(2):
            qfh[h, rows, :], qfl[h, rows, :] = qf[h]
            kfh[h, rows, :], kfl[h, rows, :] = kf[h]
            va = wide(jnp.where(lane < 64, swap_halves(v) if h else v, ones))
            a = split(dot3(qf[h], kf[h], NT) * masks[c])
            ah[h, rows, :], al[h, rows, :] = a
            num = fold(dot(a[0], va)) + dot(a[1], va[:, :128])
            if c > 0:
                hi, lo = split(state[h])
                gap = jnp.zeros((48, m), bf16)
                both = jnp.concatenate([hi, gap, lo, gap], 0)
                num = num + cont[0] * (fold(dot(qf[h][0], both, NT)) + dot(qf[h][1], both[:128], NT))
            if c < chunks - 1:
                vat = with_row(vt[h * 64 : (h + 1) * 64], 1.0, 0)
                fresh = dot3(split(vat * tail[1]), kf[h])
                state[h] = fresh if c == 0 else fresh + carry * state[h]
                sp[h, c] = stack_rows(state[h], (0, 1, 0))
            nums.append(num)
        inv = [1.0 / num[:, 64:65] for num in nums]
        mixed[rows, :] = jnp.where(lane < 64, nums[0] * inv[0], swap_halves(nums[1] * inv[1]))
        invt[rows, :] = jnp.where(lane < 64, inv[0], inv[1])


def flat_put(flat, start, value):
    tiles = value.shape[0] // 8
    for j in range(value.shape[1] // 128):
        flat[start + j * tiles : start + (j + 1) * tiles] = value[:, j * 128 : (j + 1) * 128].reshape(tiles, 8, 128)


def wout_rows(wout_s, wout_o):
    s, o = wout_s[...], wout_o[...]
    parts = [w[i : i + 128] for i in range(0, s.shape[0], 128) for w in (s, o)]
    return split(jnp.concatenate(parts, 0))


class Sum:
    def __init__(self, total, landed, done, send, recv, me, bits, polls, first=0, last=8):
        self.total, self.landed, self.done = total, landed, done
        self.send, self.recv, self.me, self.bits, self.polls = send, recv, me, bits, polls
        self.first, self.last = first * 2 * bits // 8, last * 2 * bits // 8
        units = done.shape[0] >> bits
        self.parts = []
        base = 0
        for i in range(3):
            n = ((units * (i + 1)) // 3 - (units * i) // 3) << bits
            if n:
                turn = [0, (bits + 1) // 4, (bits + 1) * 2 // 4][i]
                low = list(range(bits - 1))
                self.parts.append((base, n, low[turn:] + low[:turn] + [bits - 1], i))
            base += n

    def offset(self, part, step):
        base, n, order, _ = part
        for k in range(step):
            base = base + ((self.me >> order[k]) & 1) * (n >> (k + 1))
        return base

    def halving(self, part, step):
        base, n, order, i = part
        half = n >> (step + 1)
        mine = (self.me >> order[step]) & 1
        return pltpu.make_async_remote_copy(
            src_ref=self.total.at[pl.ds(self.offset(part, step) + (1 - mine) * half, half)],
            dst_ref=self.landed.at[pl.ds(base + n - (n >> step), half)],
            send_sem=self.send.at[i, step],
            recv_sem=self.recv.at[i, step],
            device_id={"dp": self.me ^ (1 << order[step])},
            device_id_type=MESH,
        )

    def add(self, part, step):
        base, n, order, _ = part
        half = n >> (step + 1)
        mine = (self.me >> order[step]) & 1
        keep = pl.ds(self.offset(part, step) + mine * half, half)
        to = self.done if step == self.bits - 1 else self.total
        to[keep] = self.total[keep] + self.landed[pl.ds(base + n - (n >> step), half)]

    def doubling(self, part, step):
        _, n, order, i = part
        at = pl.ds(self.offset(part, step + 1), n >> (step + 1))
        return pltpu.make_async_remote_copy(
            src_ref=self.done.at[at],
            dst_ref=self.done.at[at],
            send_sem=self.send.at[i, self.bits + step],
            recv_sem=self.recv.at[i, self.bits + step],
            device_id={"dp": self.me ^ (1 << order[step])},
            device_id_type=MESH,
        )

    def event(self, part, k):
        bits = self.bits
        end, begin = k > self.first, k < self.last
        if end and 0 < k <= bits:
            self.halving(part, k - 1).wait()
            self.add(part, k - 1)
        if end and k > bits:
            self.doubling(part, 2 * bits - k).wait()
        if begin and k < bits:
            self.halving(part, k).start()
        elif begin and k < 2 * bits:
            self.doubling(part, 2 * bits - k - 1).start()

    def due(self, q):
        todo = []
        for k in range(self.first, self.last + 1):
            at = self.polls[min(8, (k * 8 + 2 * self.bits - 1) // (2 * self.bits))]
            if at == q:
                todo += [(self, p, k) for p in self.parts]
        return todo


def greet(dp, flips, other):
    barrier = pltpu.get_barrier_semaphore()
    for flip in flips:
        pl.semaphore_signal(barrier, inc=1, device_id={"dp": dp ^ flip}, device_id_type=MESH)
    pl.semaphore_signal(barrier, inc=1, device_id=other, device_id_type=MESH)
    pl.semaphore_wait(barrier, len(flips) + 1)


def unpack(flat, start, shape, out, sem):
    tiles = shape[0] // 8
    return [
        pltpu.make_async_copy(
            flat.at[start + j * tiles : start + (j + 1) * tiles].reshape(shape[0], 128), out.at[:, j * 128 : (j + 1) * 128], sem.at[j]
        )
        for j in range(shape[1] // 128)
    ]


FFN_POLLS = (
    [6, 9, 11, 13, 15, 17, 19, 21, 24],
    [12, 15, 17, 19, 21, 24, 25],
    [18, 21, 23, 24, 25],
    [24, 25],
)
FFN_LAST = (8, 6, 4, 1)


def ffn(
    bits,
    wout_s, wout_o, gain, shift, back_bias, win_s, bin_s, wback_s, win_o, bin_o, wback_o,
    x, mixed, cot,
    out, gmid, gmix, gout, smalls, gback0, gin0, sums_left,
    mixv, cotv, middle, acc, gacc, n2h, n2l, coth, cotl, hh, hl, ph, plo,
    both, arrived, landed, done, gbin,
    load, store, mp_ss, mp_rs, ss, rs,
):
    i = pl.program_id(0)
    steps = pl.num_programs(0)
    tokens, d = x.shape
    dp = lax.axis_index("dp")
    other = {"mp": 1 - lax.axis_index("mp")}
    theirs, mine = both.at[0], both.at[1]
    groups = both.shape[1]
    sums = [
        Sum(mine.at[j], landed.at[j], done.at[j], ss.at[j], rs.at[j], dp, bits, FFN_POLLS[j], 0, FFN_LAST[j])
        for j in range(groups)
    ]

    def swap(j):
        return pltpu.make_async_remote_copy(
            src_ref=theirs.at[j], dst_ref=arrived.at[j], send_sem=mp_ss.at[j], recv_sem=mp_rs.at[j],
            device_id=other, device_id_type=MESH,
        )

    def join(j):
        swap(j).wait()
        both[1, j] = both[1, j] + arrived[j]

    def poll(q_in_step):
        for step in range(8):
            q = 3 * step + q_in_step
            todo = [e for one in sums for e in one.due(q)]
            if not todo:
                continue

            @pl.when(i == step)
            def _():
                run(todo)

    def run(todo):
        for one, p, k in todo:
            if k == 0 and p is one.parts[0]:
                join(sums.index(one))
            one.event(p, k)

    @pl.when(i == 0)
    def _():
        loads = [
            [
                pltpu.make_async_copy(src.at[t * C : (t + 1) * C], dst.at[t * C : (t + 1) * C], load.at[k, t])
                for k, (src, dst) in enumerate(((x, acc), (mixed, mixv), (cot, cotv)))
            ]
            for t in range(tokens // C)
        ]
        for copies in loads:
            for copy in copies:
                copy.start()
        greet(dp, [1 << b for b in range(bits)], other)
        wo = wout_rows(wout_s, wout_o)
        for t in range(tokens // C):
            for copy in loads[t]:
                copy.wait()
            rows = pl.ds(t * C, C)
            mid = acc[rows, :] + dot3(split(mixv[rows, :]), wo)
            middle[rows, :] = mid
            n, _ = stats(mid)
            n2h[rows, :], n2l[rows, :] = split(n * gain[...] + shift[...])
            coth[rows, :], cotl[rows, :] = split(cotv[rows, :])
            acc[rows, :] = jnp.zeros_like(mid)
            gacc[rows, :] = jnp.zeros_like(mid)

    poll(0)
    bias = jnp.where(i % 2 == 0, bin_s[...], bin_o[...])
    wi = split(jnp.where(i % 2 == 0, win_s[...], win_o[...]))
    wb = split(jnp.where(i % 2 == 0, wback_s[...], wback_o[...]))
    c0 = 0.7978845608028654
    gb = jnp.zeros((1, BH), f32)
    for t in range(tokens // C):
        if t == tokens // C // 2:
            poll(1)
        rows = pl.ds(t * C, C)
        n2 = (n2h[rows, :], n2l[rows, :])
        ct = (coth[rows, :], cotl[rows, :])
        u = dot3(n2, wi) + bias
        gh = dot3(ct, wb, NT)
        u2 = u * u
        th = jnp.tanh(c0 * (u + 0.044715 * (u2 * u)))
        hid = split(0.5 * u * (1.0 + th))
        slope = 0.5 * (1.0 + th) + 0.5 * u * (1.0 - th * th) * (c0 * (1.0 + 0.134145 * u2))
        gp = gh * slope
        gb = gb + jnp.sum(gp, 0, keepdims=True)
        gpre = split(gp)
        hh[rows, :], hl[rows, :] = hid
        ph[rows, :], plo[rows, :] = gpre
        acc[rows, :] = acc[rows, :] + dot3(hid, wb)
        gacc[rows, :] = gacc[rows, :] + dot3(gpre, wi, NT)
    gbin[pl.ds(i, 1), :] = gb
    poll(2)
    j = i // 2
    flat = both.at[i % 2, j]
    for m in range(d // C):
        cols = pl.ds(m * C, C)
        flat_put(flat, m * BH * C // 1024, dot3((hh[...], hl[...]), (coth[:, cols], cotl[:, cols]), TN))
    for m in range(BH // C):
        cols = pl.ds(m * C, C)
        flat_put(flat, d * BH // 1024 + m * d * C // 1024, dot3((n2h[...], n2l[...]), (ph[:, cols], plo[:, cols]), TN))

    @pl.when(i % 2 == 0)
    def _():
        swap(j).start()

    @pl.when(i == steps - 1)
    def _():
        run([e for one in sums for e in one.due(24)])
        wo = wout_rows(wout_s, wout_o)
        gg = jnp.zeros((1, d), f32)
        gs = gg
        gbb = gg
        stores = []
        for t in range(tokens // C):
            rows = pl.ds(t * C, C)
            mid = middle[rows, :]
            ct = cotv[rows, :]
            acc[rows, :] = mid + acc[rows, :] + back_bias[...]
            n, rsq = stats(mid)
            e = gacc[rows, :]
            gg = gg + jnp.sum(e * n, 0, keepdims=True)
            gs = gs + jnp.sum(e, 0, keepdims=True)
            gbb = gbb + jnp.sum(ct, 0, keepdims=True)
            eg = e * gain[...]
            gm = ct + rsq * (eg - jnp.mean(eg, -1, keepdims=True) - n * jnp.mean(eg * n, -1, keepdims=True))
            gacc[rows, :] = gm
            g = split(gm)
            n2h[rows, :], n2l[rows, :] = g
            coth[rows, :], cotl[rows, :] = split(mixv[rows, :])
            mixv[rows, :] = dot3(g, wo, NT)
            for k, (src, dst) in enumerate(((acc, out), (gacc, gmid), (mixv, gmix))):
                stores.append(pltpu.make_async_copy(src.at[t * C : (t + 1) * C], dst.at[t * C : (t + 1) * C], load.at[k, t]))
                stores[-1].start()
        go = dot3((coth[...], cotl[...]), (n2h[...], n2l[...]), TN)
        for slot in range(go.shape[0] // 128):
            flat_put(gout.at[slot % 2], slot // 2 * d // 8, go[slot * 128 : (slot + 1) * 128])
        for parity in range(2):
            smalls[parity, 0:2] = jnp.zeros((2, d), f32)
            smalls[parity, 2:3] = gg
            smalls[parity, 3:4] = gs
            smalls[parity, 4:5] = gbb
            used = groups * BH // d
            for r in range(used):
                per = d // BH
                smalls[parity, 5 + r : 6 + r] = jnp.concatenate(
                    [gbin[2 * (r * per + c) + parity : 2 * (r * per + c) + parity + 1] for c in range(per)], 1
                )
            if used < 3:
                smalls[parity, 5 + used :] = jnp.zeros((3 - used, d), f32)
        last = unpack(done.at[0], 0, (BH, d), gback0, store.at[0:6]) + unpack(
            done.at[0], d * BH // 1024, (d, BH), gin0, store.at[6:12]
        )
        for copy in last:
            copy.start()
        run([e for one in sums for e in one.due(25)])
        for g in range(1, groups):
            left = done if sums[g].last >= bits else both.at[1]
            last.append(pltpu.make_async_copy(left.at[g], sums_left.at[g - 1], store.at[11 + g]))
            last[-1].start()
        for copy in stores + last:
            copy.wait()


POLLS = 4
BWD_POLLS = (
    [0, 0, 0, 0, 0, 0, 0, 3, 5],
    [0, 0, 0, 0, 0, 3, 5, 7, 9],
    [0, 0, 3, 5, 7, 9, 11, 13, 15],
    [3, 5, 7, 9, 11, 13, 15, 16, 16],
    [8, 11, 13, 15, 16, 16, 16, 16, 16],
    None,
)


def small_stages(bits):
    return [(shift, min(2, bits - shift)) for shift in range(0, bits, 2)]


def attn_bwd(
    bits,
    gain, shift, segs, fback, gm, mixed, invt, sq, sk, vv, qfh, qfl, kfh, kfl, ah, al, sp, small,
    x, gmid, w_hi, w_lo, sums_left, gout,
    ginputs, gback1, gin1, gout_out, qkv0, qkv1, smalls,
    n1h, n1l, xv, gv, wh, wl, gh, gl, masks, segc, segr,
    done, ffn, ffn_in, heads, heads_send, heads_mp, heads_in, heads_done, outs, outs_send, outs_mp, outs_in, outs_done,
    sm, sm_in,
    load, store, ss, rs, mp_ss, mp_rs, sm_ss, sm_rs,
):
    slot = pl.program_id(0)
    slots = pl.num_programs(0)
    tokens, d = x.shape
    chunks = tokens // C
    scale = 64.0 ** -0.25
    dp = lax.axis_index("dp")
    other = {"mp": 1 - lax.axis_index("mp")}
    gtiles = gout.shape[1]
    qtiles = d // 8
    left = sums_left.shape[0]
    stages = small_stages(bits)
    polled = [
        Sum(ffn if FFN_LAST[j + 1] * 2 * bits // 8 < bits else None, ffn_in, done.at[j], ss.at[j], rs.at[j], dp, bits,
            BWD_POLLS[j], FFN_LAST[j + 1])
        for j in range(left)
    ]
    outs_sum = Sum(outs, outs_in, outs_done, ss.at[left], rs.at[left], dp, bits, BWD_POLLS[left])
    half_sum, tail_sum = (
        Sum(heads.at[j], heads_in.at[j], heads_done.at[j], ss.at[left + 1 + j], rs.at[left + 1 + j], dp, bits, BWD_POLLS[left + 1 + j])
        for j in range(2)
    )
    polled += [outs_sum, half_sum]

    def to_sibling(src, dst, i):
        return pltpu.make_async_remote_copy(
            src_ref=src, dst_ref=dst, send_sem=mp_ss.at[i], recv_sem=mp_rs.at[i], device_id=other, device_id_type=MESH
        )

    swap_out = to_sibling(outs_send, outs_mp, 0)
    swap_heads = [to_sibling(heads_send.at[j], heads_mp.at[j], 1 + j) for j in range(2)]
    loads = [
        pltpu.make_async_copy(*pair, load.at[i])
        for i, pair in enumerate((
            (x, xv), (gout.at[0], outs_send), (gout.at[1], outs.at[0:gtiles]),
            (w_hi, wh), (w_lo, wl), (gmid, gv),
        ))
    ]
    resumes = [
        pltpu.make_async_copy(sums_left.at[j], done.at[j] if polled[j].total is None else ffn, load.at[6 + j])
        for j in range(left)
    ]

    def run(todo):
        for one, p, k in todo:
            if one is outs_sum and k == 0 and p is one.parts[0]:
                swap_out.wait()
                outs[0:gtiles] = outs[0:gtiles] + outs_mp[...]
            one.event(p, k)

    def due(q):
        return [e for one in polled for e in one.due(q)]

    def poll(q_in_slot):
        for step in range(4):
            todo = due(step * POLLS + q_in_slot)
            if todo:

                @pl.when(slot == step)
                def _():
                    run(todo)

    @pl.when(slot == 0)
    def _():
        for copy in resumes + loads:
            copy.start()
        for copy in resumes:
            copy.wait()
        greet(dp, sorted({1 << b for b in range(bits)} | {j << s for s, w in stages for j in range(1, 1 << w)}), other)
        make_masks(masks, segc, segr, segs)
        for r, used in ((outs, gtiles), (heads.at[0], 3 * qtiles), (heads.at[1], 3 * qtiles)):
            if used < r.shape[0]:
                r[used:] = jnp.zeros((r.shape[0] - used, 8, 128), f32)
        for copy in loads[:3]:
            copy.wait()
        swap_out.start()

    @pl.when(slot == 0)
    def _():
        for c in range(chunks):
            rows = pl.ds(c * C, C)
            n, _ = stats(xv[rows, :])
            n1h[:, rows], n1l[:, rows] = split((n * gain[...] + shift[...]).T)

    lane = lanes(C)
    at = pl.ds(pl.multiple_of(slot * 128, 128), 128)
    keys_one = jnp.where((lane == 64) | (lane == 66), 1.0, 0.0)

    def put(which, rows, g):
        gh[which, rows, at], gl[which, rows, at] = split(g)

    def back(which, rows, grads, feats, s):
        total = None
        sums = []
        for h in range(2):
            dd = grads[h] * (feats[h][0].astype(f32) + feats[h][1].astype(f32))
            sums.append(jnp.sum(dd, -1, keepdims=True))
            for half in split(dd):
                term = dot(half, fback[h], NT)
                total = term if total is None else total + term
        put(which, rows, (fold(total) - s * jnp.where(lane < 64, sums[0], sums[1])) * scale)

    grad = [None, None]
    for c in reversed(range(chunks)):
        poll(chunks - 1 - c)
        rows = pl.ds(c * C, C)
        cont, tailk, carry = seg_flags(segc, segr, c)
        u = gm[rows, :] * invt[rows, :]
        prod = u * mixed[rows, :]
        weights = [-jnp.sum(jnp.where(lane // 64 == h, prod, 0.0), -1, keepdims=True) for h in range(2)]
        ut = u.T
        wt = jnp.where(lane < 64, weights[0], weights[1]).T
        ru = right_pack(u, weights, lane)
        lv = left_pack(vv[rows, :], keys_one, lane)
        gq, gk, gvt, qfs, kfs = [], [], [], [], []
        for h in range(2):
            qf = (qfh[h, rows, :], qfl[h, rows, :])
            kf = (kfh[h, rows, :], kfl[h, rows, :])
            ga = split(dot(ru[h], lv[h], NT) * masks[c])
            gqf = dot3(ga, kf)
            gkf = dot3(ga, qf, TN)
            uth = ut[h * 64 : (h + 1) * 64]
            gvh = dot3(split(uth), (ah[h, rows, :], al[h, rows, :]))
            if c > 0:
                gqf = gqf + cont[0] * dot(ru[h], sp[h, c - 1])
            if c < chunks - 1:
                gkf = gkf + tailk[0] * dot(lv[h], stack_rows(grad[h], (0, 0, 1)))
                gvh = gvh + tailk[1] * dot3(split(grad[h][:64]), kf, NT)
            if c > 0:
                fresh = dot3(split(with_row(uth, wt[h * 64 : h * 64 + 1], 0) * cont[1]), qf)
                grad[h] = fresh if c == chunks - 1 else fresh + carry * grad[h]
            gq.append(gqf)
            gk.append(gkf)
            gvt.append(gvh)
            qfs.append(qf)
            kfs.append(kf)
        back(0, rows, gq, qfs, sq[rows, :])
        back(1, rows, gk, kfs, sk[rows, :])
        put(2, rows, jnp.concatenate(gvt, 0).T)

    def weight_grads(flat):
        g = dot3(
            (n1h[...], n1l[...]), [jnp.concatenate([r[i, :, at] for i in range(3)], 1) for r in (gh, gl)]
        )
        flat_put(flat, 0, g)

    for j in range(2):

        @pl.when(slot == 2 * j)
        def _():
            weight_grads(heads_send.at[j])
            swap_heads[j].start()

    def own_grads(j):
        weight_grads(heads.at[j])
        swap_heads[j].wait()
        used = 3 * qtiles
        heads[j, 0:used] = heads[j, 0:used] + heads_mp[j]

    @pl.when(slot == 1)
    def _():
        own_grads(0)

    @pl.when(slot == slots - 1)
    def _():
        own_grads(1)
        run([(tail_sum, p, 0) for p in tail_sum.parts])
        for copy in loads[3:]:
            copy.wait()
        run([e for one in polled[:left] for e in one.due(16)])
        waiting = [[[e for e in one.due(16) if e[2] == k] for k in range(2 * bits + 1)] for one in polled[left:]]
        waiting = [[e for e in chain if e] for chain in waiting]
        following = [[(tail_sum, p, k) for p in tail_sum.parts] for k in range(1, 2 * bits + 1)]

        def half_next():
            for chain in waiting:
                if chain:
                    run(chain.pop(0))

        def tail_next():
            if following:
                run(following.pop(0))

        stores = []
        for g in range(left):
            stores += unpack(done.at[g], 0, (BH, d), gback1.at[g * BH : (g + 1) * BH], store.at[12 * g : 12 * g + 6])
            stores += unpack(
                done.at[g], d * BH // 1024, (d, BH), gin1.at[:, g * BH : (g + 1) * BH], store.at[12 * g + 6 : 12 * g + 12]
            )
        for copy in stores:
            copy.start()
        half_next()
        gg = jnp.zeros((1, d), f32)
        gs = gg
        for c in range(chunks):
            rows = pl.ds(c * C, C)
            n, rsq = stats(xv[rows, :])
            e = jnp.zeros((C, d), f32)
            for i in range(3):
                e = e + dot3((gh[i, rows, :], gl[i, rows, :]), (wh[i], wl[i]), NT)
            gg = gg + jnp.sum(e * n, 0, keepdims=True)
            gs = gs + jnp.sum(e, 0, keepdims=True)
            eg = e * gain[...]
            gv[rows, :] = gv[rows, :] + rsq * (
                eg - jnp.mean(eg, -1, keepdims=True) - n * jnp.mean(eg * n, -1, keepdims=True)
            )
            tail_next()
            half_next()
        rows_store = [pltpu.make_async_copy(gv, ginputs, store.at[12 * left])]
        rows_store[0].start()
        sm[0] = jnp.concatenate([gg, gs, small[0, 2:]], 0)
        first = to_sibling(sm.at[0], sm_in.at[0], 3)
        first.start()
        tail_next()
        while any(waiting):
            half_next()
        base = 12 * left + 1
        for s in range(gtiles * 8 // d):
            rows_store += unpack(
                outs_done, s * d // 8, (128, d), gout_out.at[s * 128 : (s + 1) * 128], store.at[base + 4 * s : base + 4 * s + 4]
            )
        base += gtiles * 32 // d
        for c in range(3):
            rows_store += unpack(heads_done.at[0], c * qtiles, (d, 128), qkv0.at[c], store.at[base + c : base + c + 1])
        for copy in rows_store[1:]:
            copy.start()
        first.wait()
        sm[1] = jnp.concatenate([gg, gs, small[1, 2:]], 0) + sm_in[0]
        for i, (shift, width) in enumerate(stages):
            digit = (dp >> shift) & ((1 << width) - 1)
            sends = [
                pltpu.make_async_remote_copy(
                    src_ref=sm.at[i + 1], dst_ref=sm_in.at[1 + 4 * i + digit], send_sem=sm_ss.at[3 * i + j - 1],
                    recv_sem=sm_rs.at[3 * i + j - 1], device_id={"dp": dp ^ (j << shift)}, device_id_type=MESH,
                )
                for j in range(1, 1 << width)
            ]
            for copy in sends:
                copy.start()
            sm_in[1 + 4 * i + digit] = sm[i + 1]
            tail_next()
            for copy in sends:
                copy.wait()
            total = sm_in[1 + 4 * i]
            for j in range(1, 1 << width):
                total = total + sm_in[1 + 4 * i + j]
            sm[i + 2] = total
        while following:
            tail_next()
        smalls[...] = sm[len(stages) + 1]
        ends = []
        base += 3
        for c in range(3):
            ends += unpack(heads_done.at[1], c * qtiles, (d, 128), qkv1.at[c], store.at[base + c : base + c + 1])
        for copy in ends:
            copy.start()
        for copy in stores + rows_store + ends:
            copy.wait()


def whole(shape):
    return pl.BlockSpec(shape, lambda i: (0,) * len(shape))


def params(**more):
    return pltpu.CompilerParams(vmem_limit_bytes=VMEM_LIMIT, dimension_semantics=("arbitrary",), **more)


def sds(shape, dtype=f32):
    return jax.ShapeDtypeStruct(shape, dtype)


ANY = pl.BlockSpec(memory_space=pl.ANY)


def run_attn_fwd(x, gain, shift, segs, w, features):
    t, d = x.shape
    heads, _, m = features.shape
    cols = w.shape[2]
    chunks = t // C
    slot = lambda i: (i % 2) * 2 + 1 - i // 2
    per_pair = pl.BlockSpec((t, 128), lambda i: (0, slot(i)))
    per_head = pl.BlockSpec((2, t, m), lambda i: (slot(i), 0, 0))
    sem = lambda *n: pltpu.SemaphoreType.DMA(n)
    return pl.pallas_call(
        attn_fwd,
        grid=(heads,),
        in_specs=[whole((t, d)), whole((1, d)), whole((1, d)), whole(segs.shape), ANY, ANY],
        out_specs=[per_pair] * 3 + [per_head] * 4 + [pl.BlockSpec((2, t, C), lambda i: (slot(i), 0, 0))] * 2
        + [pl.BlockSpec((2, chunks - 1, 256, m), lambda i: (slot(i), 0, 0, 0))] + [per_pair] * 2
        + [pl.BlockSpec((2, 256, m), lambda i: (slot(i), 0, 0))] + [pl.BlockSpec((3, d, 128), lambda i: (0, 0, slot(i)))] * 2,
        out_shape=[sds((t, 2 * cols))] * 3 + [sds((2 * heads, t, m), bf16)] * 4 + [sds((2 * heads, t, C), bf16)] * 2
        + [sds((2 * heads, chunks - 1, 256, m), bf16)] + [sds((t, 2 * cols))] * 2 + [sds((2 * heads, 256, m), bf16)]
        + [sds((3, d, 2 * cols), bf16)] * 2,
        scratch_shapes=[pltpu.VMEM((t, cols), f32)] * 3 + [pltpu.VMEM((t, d), bf16)] * 2 + [pltpu.VMEM((chunks, C, C), f32)]
        + [pltpu.VMEM((t, 128), f32), pltpu.VMEM((1, t), f32)] + [pltpu.VMEM((2,) + w.shape, f32), pltpu.VMEM((2,) + features.shape, f32), sem(2), sem(2), sem(2)],
        cost_estimate=pl.CostEstimate(flops=60 * t * d * d, bytes_accessed=80 * t * d * 4, transcendentals=2 * t * d),
        compiler_params=params(collective_id=3, has_side_effects=True),
        name="attn_fwd",
    )(x, gain, shift, segs, w, features)


def run_ffn(x, mixed, wout_s, wout_o, gain, shift, back_bias, cot, w_s, w_o, dp_size):
    t, d = x.shape
    hid = w_s[0].shape[1]
    cols = mixed.shape[1]
    bits = dp_size.bit_length() - 1
    groups = hid // BH
    tiles = 2 * d * BH // 1024
    weights = [
        pl.BlockSpec((d, BH), lambda i: (0, i // 2)), pl.BlockSpec((1, BH), lambda i: (0, i // 2)),
        pl.BlockSpec((BH, d), lambda i: (i // 2, 0)),
    ]
    half = (2, cols // 2 * d // 1024, 8, 128)
    sem = lambda *n: pltpu.SemaphoreType.DMA(n)
    vm = lambda shape, dtype=f32: pltpu.VMEM(shape, dtype)
    block = (groups, tiles, 8, 128)
    return pl.pallas_call(
        functools.partial(ffn, bits),
        grid=(2 * groups,),
        in_specs=[whole(wout_s.shape), whole(wout_o.shape)] + [whole((1, d))] * 3 + weights * 2 + [ANY] * 3,
        out_specs=[ANY] * 3 + [whole(half), whole((2, 8, d))] + [ANY] * 3,
        out_shape=[sds((t, d)), sds((t, d)), sds((t, cols)), sds(half), sds((2, 8, d)),
                   sds((BH, d)), sds((d, BH)), sds((groups - 1,) + block[1:])],
        scratch_shapes=[vm((t, cols)), vm((t, d)), vm((t, d)), vm((t, d)), vm((t, d))] + [vm((t, d), bf16)] * 4
        + [vm((t, BH), bf16)] * 4
        + [vm((2,) + block), vm(block)] + [vm(block)] * 2 + [vm((2 * groups, BH))]
        + [sem(3, t // C), sem(11 + groups), sem(groups), sem(groups), sem(groups, 3, 2 * bits), sem(groups, 3, 2 * bits)],
        compiler_params=params(collective_id=1, has_side_effects=True),
        name="ffn",
    )(wout_s, wout_o, gain, shift, back_bias, *w_s, *w_o, x, mixed, cot)


def run_attn_bwd(x, gain, shift, segs, gm, saved, small, gmid, sums_left, gout, dp_size):
    sq, sk, vv, qfh, qfl, kfh, kfl, ah, al, sp, mixed, invt, fback, wh, wl = saved
    t, d = x.shape
    heads, _, m = fback.shape
    cols = gm.shape[1]
    chunks = t // C
    bits = dp_size.bit_length() - 1
    up = lambda n: -(-n // dp_size) * dp_size
    stages = len(small_stages(bits))
    tiles = lambda n: pltpu.VMEM((n, 8, 128), f32)
    left, nf = sums_left.shape[:2]
    ng, nq = gout.shape[1], 3 * d // 8
    pair = lambda n: pltpu.VMEM((2, n, 8, 128), f32)
    sem = lambda *n: pltpu.SemaphoreType.DMA(n)
    per_slot = pl.BlockSpec((t, 128), lambda p: (0, p))
    per_head = pl.BlockSpec((2, t, m), lambda p: (p, 0, 0))
    rows = small.shape[1]
    return pl.pallas_call(
        functools.partial(attn_bwd, bits),
        grid=(heads // 2,),
        in_specs=[
            whole((1, d)), whole((1, d)), whole(segs.shape), pl.BlockSpec((2, 256, m), lambda p: (p, 0, 0)),
        ] + [per_slot] * 6 + [per_head] * 4 + [pl.BlockSpec((2, t, C), lambda p: (p, 0, 0))] * 2
        + [pl.BlockSpec((2, chunks - 1, 256, m), lambda p: (p, 0, 0, 0))] + [whole(small.shape)] + [ANY] * 6,
        out_specs=[ANY] * 6 + [whole((rows, d))],
        out_shape=[sds((t, d)), sds((left * BH, d)), sds((d, left * BH)), sds((cols // 2, d)), sds((3, d, 128)), sds((3, d, 128)),
                   sds((rows, d))],
        scratch_shapes=[pltpu.VMEM((d, t), bf16)] * 2 + [pltpu.VMEM((t, d), f32)] * 2 + [pltpu.VMEM((3, d, cols), bf16)] * 2
        + [pltpu.VMEM((3, t, cols), bf16)] * 2 + [pltpu.VMEM((chunks, C, C), f32), pltpu.VMEM((t, 128), f32), pltpu.VMEM((1, t), f32)]
        + [pltpu.VMEM((left, nf, 8, 128), f32), tiles(nf), tiles(nf)] + [pair(up(nq)), pair(nq), pair(nq), pair(up(nq)), pair(up(nq))]
        + [tiles(up(ng)), tiles(ng), tiles(ng), tiles(up(ng)), tiles(up(ng))]
        + [pltpu.VMEM((stages + 2, rows, d), f32), pltpu.VMEM((4 * stages + 1, rows, d), f32)]
        + [sem(6 + left), sem(12 * left + 1 + ng * 32 // d + 6), sem(left + 3, 3, 2 * bits), sem(left + 3, 3, 2 * bits), sem(4), sem(4), sem(3 * stages), sem(3 * stages)],
        compiler_params=params(collective_id=2, has_side_effects=True),
        name="attn_bwd",
    )(gain, shift, segs, fback, gm, mixed, invt, sq, sk, vv, qfh, qfl, kfh, kfl, ah, al, sp, small,
      x, gmid, wh, wl, sums_left, gout)


def place(output, ginputs, gback0, gback1, gin0, gin1, gout, qkv0, qkv1, small, o1, o2, o3, o4, o5, o6, obias, *vectors):
    used = obias.shape[0] // small.shape[1]
    for r in range(used):
        obias[r * small.shape[1] : (r + 1) * small.shape[1]] = small[5 + r]
    for r, vector in enumerate(vectors):
        vector[...] = small[r]
    o1[...] = output[...]
    o2[...] = ginputs[...]
    o4[:, : gin0.shape[1]] = gin0[...]
    o4[:, gin0.shape[1] :] = gin1[...]
    o5[...] = gout[...]
    o6[:, :, :128] = qkv0[...]
    o6[:, :, 128:] = qkv1[...]
    first = pl.program_id(0) * o3.shape[0] < BH

    @pl.when(first)
    def _():
        o3[...] = gback0[...]

    @pl.when(jnp.logical_not(first))
    def _():
        o3[...] = gback1[...]


def run_place(output, ginputs, gback0, gback1, gin0, gin1, gout, qkv0, qkv1, small):
    steps = 4
    back = (gback0.shape[0] + gback1.shape[0], gback0.shape[1])
    ins = (gin0.shape[0], gin0.shape[1] + gin1.shape[1])
    qkv = qkv0.shape[:2] + (2 * qkv0.shape[2],)
    rows = lambda shape: pl.BlockSpec((shape[0] // steps, shape[1]), lambda i: (i, 0))
    mids = lambda shape: pl.BlockSpec((shape[0], shape[1] // steps, shape[2]), lambda i: (0, i, 0))
    size = back[0] // steps
    n0 = gback0.shape[0] // size
    return pl.pallas_call(
        place,
        grid=(steps,),
        in_specs=[
            rows(output.shape), rows(ginputs.shape),
            pl.BlockSpec((size, back[1]), lambda i: (jnp.minimum(i, n0 - 1), 0)),
            pl.BlockSpec((size, back[1]), lambda i: (jnp.maximum(i - n0, 0), 0)),
            rows(gin0.shape), rows(gin1.shape), rows(gout.shape), mids(qkv0.shape), mids(qkv1.shape), whole(small.shape),
        ],
        out_specs=[rows(output.shape), rows(ginputs.shape), rows(back), rows(ins), rows(gout.shape), mids(qkv), whole(back[:1])] + [whole(back[1:])] * 5,
        out_shape=[sds(output.shape), sds(ginputs.shape), sds(back), sds(ins), sds(gout.shape), sds(qkv), sds(back[:1])] + [sds(back[1:])] * 5,
        compiler_params=params(),
        name="place",
    )(output, ginputs, gback0, gback1, gin0, gin1, gout, qkv0, qkv1, small)


def body(
    dp_size,
    inputs, segment_ids, first_gain, first_shift, qkv_weight, out_weight, features,
    second_gain, second_shift, in_weight, in_bias, back_weight, back_bias, cotangent,
):
    swap = [(0, 1), (1, 0)]

    def other(array):
        return lax.ppermute(array, "mp", swap)

    row = lambda v: v.reshape(1, -1)
    out_s = other(out_weight)
    in_s, bin_s, back_s = other(in_weight), other(in_bias), other(back_weight)
    g1, s1, g2, s2 = row(first_gain), row(first_shift), row(second_gain), row(second_shift)
    saved = run_attn_fwd(inputs, g1, s1, segment_ids, qkv_weight, features.swapaxes(1, 2))
    output, gmid, gmix, gout, small, gback0, gin0, sums_left = run_ffn(
        inputs, saved[10], out_s, out_weight, g2, s2, row(back_bias), cotangent,
        (in_s, row(bin_s), back_s), (in_weight, row(in_bias), back_weight), dp_size,
    )
    g_inputs, gback1, gin1, g_out, qkv0, qkv1, small = run_attn_bwd(
        inputs, g1, s1, segment_ids, gmix, saved, small, gmid, sums_left, gout, dp_size,
    )
    output, g_inputs, gback, gin, g_out, gqkv, gbin, *small = run_place(
        output, g_inputs, gback0, gback1, gin0, gin1, g_out, qkv0, qkv1, small
    )
    return (output, g_inputs, small[0], small[1], gqkv, g_out, small[2], small[3], gin, gbin, gback, small[4])


def solution(mesh):
    rows = P(("dp", "mp"), None)
    return jax.shard_map(
        functools.partial(body, mesh.shape["dp"]),
        mesh=mesh,
        in_specs=(
            rows, P("dp", None), P(), P(), P(None, None, "mp"), P("mp", None), P("mp", None, None),
            P(), P(), P(None, "mp"), P("mp"), P("mp", None), P(), rows,
        ),
        out_specs=(
            rows, rows, P(), P(), P(None, None, "mp"), P("mp", None), P(), P(), P(None, "mp"), P("mp"), P("mp", None), P(),
        ),
        check_vma=False,
    )
```

time: 979 us -> 235 us (0.24)
  matrix products: 426 us -> 0 us
  Pallas kernels: 0 us -> 231 us
  waiting for transfers between devices: 209 us -> 0.01 us
  local copies, waits for them, and re-layouts: 115 us -> 1.46 us
  other arithmetic: 88.7 us -> 0 us
  blocking collectives: 85.3 us -> 0 us
  loops' own time: 31.7 us -> 0 us
  between operations: 14.8 us -> 0.94 us
    dot_general x44 -> x0, matrix products: 426 us -> none  [the longest x6 71.2 us: advance(): jnp.einsum('rihm,rjhm->rhij', query_block, key_block, precision=top_preci...]
    pallas_call x0 -> x4, Pallas kernels: none -> 231 us  [the longest x1 108 us: run_attn_bwd(): pl.pallas_call(functools.partial(attn_bwd, bits), grid=(heads // 2,), in_...]
    psum x1 -> x0, waiting for transfers between devices: 145 us -> none  [body(): lax.psum((g_qkv_weight, g_out_weight, input_weight_gradient, g_in_bias, g...]
    psum x2 -> x0, blocking collectives: 85.3 us -> none  [the longest x1 44.5 us: body(): lax.psum((g_qkv_weight, g_out_weight, input_weight_gradient, g_in_bias, g...]
    reduce_sum x16 -> x0, other arithmetic: 41.7 us -> none  [the longest x1 13.5 us: feature_map(): project_rows - 0.5 * jnp.sum(scaled_values * scaled_values, -1, keepdims=...]
    reduce_scatter x4 -> x0, waiting for transfers between devices: 32.5 us -> none  [the longest x1 13.3 us: body(): lax.psum_scatter(attn_terms, 'mp', scatter_dimension=0, tiled=True)]
    another operation x2 -> x0, loops' own time: 31.7 us -> none  [block_attend(): lax.scan(advance, initial, (blockwise(query_feats), blockwise(key_feats),...]
    all_gather x4 -> x0, waiting for transfers between devices: 30.8 us -> none  [the longest x1 16.4 us: body(): first_rows = lax.all_gather(first_normed, 'mp', axis=0, tiled=True)]
  transfers between devices with their start and end apart: 9 -> 4, of which waited for: 6 -> 0; matrix products, arithmetic and copies ran while one was open for 11% -> 0% of each run, Pallas kernels for 0% -> 14%
where the time goes in v1:
time: 235 us; the launch traced here: 234 us
  Pallas kernels  231 us (98%)
    pallas_call x1, Pallas kernels, run_attn_bwd(): pl.pallas_call(functools.partial(attn_bwd, bits), grid=(heads // 2,), in_...  108 us
    pallas_call x1, Pallas kernels, run_ffn(): pl.pallas_call(functools.partial(ffn, bits), grid=(2 * groups,), in_specs...  82.1 us
    pallas_call x1, Pallas kernels, run_attn_fwd(): pl.pallas_call(attn_fwd, grid=(heads,), in_specs=[whole((t, d)), whole((1...  31.8 us
    pallas_call x1, Pallas kernels, run_place(): pl.pallas_call(place, grid=(steps,), in_specs=[rows(output.shape), rows(g...  8.3 us
  transfers between devices with their start and end apart: 4, of which 0 were waited for; matrix products, arithmetic and copies ran while one was open for 0% of the time, Pallas kernels for 14%

profile of v1, /device:TPU:0, one launch (start us, length us, event | category | flops | bytes accessed | tf_op | source)
XLA Modules:
  0.0 234.2 jit_solution(2587455432045365901)
XLA Ops:
  0.6 0.5 collective-permute-start.1
  1.2 0.1 collective-permute-start.3
  1.2 0.4 collective-permute-start.2
  1.7 0.1 collective-permute-start
  1.8 31.8 %attn_fwd.1 = (f32[1024,512]{1,0:T(8,128)}, f32[1024,512]{1,0:T(8,128)}, f32[1024,512]{1,0:T(8,128)}, bf16[8,1024,256]{2,1,0:T(8,128)(2,1)}, bf16[8,1024,256]{2,...) custom-call(f32[1024,512]{1,0:T(8,128)} %x.5, ...), custom_call_target="tpu_custom_call" | custom-call | flops 16106127360 | bytes 167772160 | tf_op jit(solution)/shard_map/attn_fwd/pallas_call | solution.py:836
  33.5 0.0 collective-permute-done.2
  33.5 0.0 copy-start.2
  33.5 0.0 collective-permute-done.wout_s
  33.5 0.0 copy-start.1
  33.6 0.0 collective-permute-done.1.win_s
  33.6 0.0 copy-start
  33.6 0.0 collective-permute-done.3.wback_s
  33.6 0.5 copy-done.2
  34.1 0.2 copy-done.1
  34.3 0.7 copy-done
  35.0 82.1 %ffn.1 = (f32[1024,512]{1,0:T(8,128)}, f32[1024,512]{1,0:T(8,128)}, f32[1024,512]{1,0:T(8,128)}, f32[2,128,8,128]{3,2,1,0:T(8,128)}, f32[2,8,512]{2,1,0:T(8,128)...) custom-call(f32[256,512]{1,0:T(8,128)} %copy-done.1, f32[256,512]{1,0:T(8,128)} %wout_o.1, ...), custom_call_target="tpu_custom_call" | custom-call | tf_op jit(solution)/shard_map/ffn/pallas_call | solution.py:869
  117.2 108.5 %attn_bwd.1 = (f32[1024,512]{1,0:T(8,128)}, f32[768,512]{1,0:T(8,128)}, f32[512,768]{1,0:T(8,128)}, f32[256,512]{1,0:T(8,128)}, f32[3,512,128]{2,1,0:T(8,128)}, ...) custom-call(f32[1,512]{1,0:T(1,128)} %bitcast.14, f32[1,512]{1,0:T(1,128)} %bitcast.16, s32[2,1024]{1,0:T(2,128)} %segs.3, ...), custom_call_target="tpu_custom_call" | custom-call | tf_op jit(solution)/shard_map/attn_bwd/pallas_call | solution.py:902
  225.7 8.3 %place.1 = (f32[1024,512]{1,0:T(8,128)}, f32[1024,512]{1,0:T(8,128)}, f32[1024,512]{1,0:T(8,128)}, f32[512,1024]{1,0:T(8,128)}, f32[256,512]{1,0:T(8,128)}, /*in...) custom-call(f32[1024,512]{1,0:T(8,128)} %get-tuple-element.55.output, ...), custom_call_target="tpu_custom_call" | custom-call | tf_op jit(solution)/shard_map/place/pallas_call | solution.py:957
Async XLA Ops:
  0.6 32.9 %collective-permute-start.1 = (f32[512,1024]{1,0:T(8,128)}, f32[512,1024]{1,0:T(8,128)S(1)}, u32[]{:S(2)}, u32[]{:S(2)}) collective-permute-start(f32[512,1024]{1,0:T(8,128)} %win_o.1), channel_id=1, source_target_pairs={{0,1},{1,0},{2,3},{3,2},{4,5},{5,4},{6,7},{7,6},{8,9},{9,8},{10,11... | collective-permute-start | bytes 6291464 | tf_op jit(solution)/shard_map/ppermute | solution.py:981
  1.2 32.4 %collective-permute-start.3 = (f32[1024,512]{1,0:T(8,128)}, f32[1024,512]{1,0:T(8,128)}, u32[]{:S(2)}, u32[]{:S(2)}) collective-permute-start(f32[1024,512]{1,0:T(8,128)} %wback_o.1), channel_id=1, source_target_pairs={{0,1},{1,0},{2,3},{3,2},{4,5},{5,4},{6,7},{7,6},{8,9},{9,8},{10,11... | collective-permute-start | bytes 6291464 | tf_op jit(solution)/shard_map/ppermute | solution.py:981
  1.2 32.3 %collective-permute-start.2 = (f32[1024]{0:T(1024)}, f32[1024]{0:T(1024)S(1)}, u32[]{:S(2)}, u32[]{:S(2)}) collective-permute-start(f32[1024]{0:T(1024)} %param.24), channel_id=1, source_target_pairs={{0,1},{1,0},{2,3},{3,2},{4,5},{5,4},{6,7},{7,6},{8,9},{9,8},{10,11... | collective-permute-start | bytes 12296 | tf_op jit(solution)/shard_map/ppermute | solution.py:981
  1.7 31.9 %collective-permute-start = (f32[256,512]{1,0:T(8,128)}, f32[256,512]{1,0:T(8,128)S(1)}, u32[]{:S(2)}, u32[]{:S(2)}) collective-permute-start(f32[256,512]{1,0:T(8,128)} %wout_o.1), channel_id=1, source_target_pairs={{0,1},{1,0},{2,3},{3,2},{4,5},{5,4},{6,7},{7,6},{8,9},{9,8},{10,11... | collective-permute-start | bytes 1572872 | tf_op jit(solution)/shard_map/ppermute | solution.py:981
  33.5 0.6 copy-start.2
  33.5 0.8 copy-start.1
  33.6 1.5 copy-start

commit v2 on v1

--- a/solution.py
+++ b/solution.py
@@ -255,10 +255,11 @@
         self.send, self.recv, self.me, self.bits, self.polls = send, recv, me, bits, polls
         self.first, self.last = first * 2 * bits // 8, last * 2 * bits // 8
         units = done.shape[0] >> bits
+        cuts = (0, units * 6 // 16, units * 12 // 16, units)
         self.parts = []
         base = 0
         for i in range(3):
-            n = ((units * (i + 1)) // 3 - (units * i) // 3) << bits
+            n = (cuts[i + 1] - cuts[i]) << bits
             if n:
                 turn = [0, (bits + 1) // 4, (bits + 1) * 2 // 4][i]
                 low = list(range(bits - 1))
@@ -345,8 +346,8 @@
 
 
 FFN_POLLS = (
-    [6, 9, 11, 13, 15, 17, 19, 21, 24],
-    [12, 15, 17, 19, 21, 24, 25],
+    [6, 10, 12, 14, 16, 18, 20, 22, 24],
+    [12, 16, 18, 20, 22, 24, 25],
     [18, 21, 23, 24, 25],
     [24, 25],
 )

time: 235 us -> 231 us (0.983)
  Pallas kernels: 231 us -> 227 us
    pallas_call x1, Pallas kernels: 82.1 us -> 78.7 us  [run_ffn(): pl.pallas_call(functools.partial(ffn, bits), grid=(2 * groups,), in_specs...]
where the time goes in v2:
time: 231 us
  Pallas kernels  227 us (98%)
    pallas_call x1, Pallas kernels, run_attn_bwd(): pl.pallas_call(functools.partial(attn_bwd, bits), grid=(heads // 2,), in_...  109 us
    pallas_call x1, Pallas kernels, run_ffn(): pl.pallas_call(functools.partial(ffn, bits), grid=(2 * groups,), in_specs...  78.7 us
    pallas_call x1, Pallas kernels, run_attn_fwd(): pl.pallas_call(attn_fwd, grid=(heads,), in_specs=[whole((t, d)), whole((1...  31.8 us
    pallas_call x1, Pallas kernels, run_place(): pl.pallas_call(place, grid=(steps,), in_specs=[rows(output.shape), rows(g...  8.3 us
  transfers between devices with their start and end apart: 4, of which 0 were waited for; matrix products, arithmetic and copies ran while one was open for 0% of the time, Pallas kernels for 14%

profile of v2, /device:TPU:0, one launch (start us, length us, event | category | flops | bytes accessed | tf_op | source)
XLA Modules:
  0.0 230.9 jit_solution(7558100684802499876)
XLA Ops:
  0.6 0.5 collective-permute-start.1
  1.2 0.1 collective-permute-start.3
  1.2 0.4 collective-permute-start.2
  1.7 0.1 collective-permute-start
  1.8 31.8 %attn_fwd.1 = (f32[1024,512]{1,0:T(8,128)}, f32[1024,512]{1,0:T(8,128)}, f32[1024,512]{1,0:T(8,128)}, bf16[8,1024,256]{2,1,0:T(8,128)(2,1)}, bf16[8,1024,256]{2,...) custom-call(f32[1024,512]{1,0:T(8,128)} %x.5, ...), custom_call_target="tpu_custom_call" | custom-call | flops 16106127360 | bytes 167772160 | tf_op jit(solution)/shard_map/attn_fwd/pallas_call | solution.py:837
  33.5 0.0 collective-permute-done.2
  33.5 0.0 copy-start.2
  33.5 0.0 collective-permute-done.wout_s
  33.5 0.0 copy-start.1
  33.6 0.0 collective-permute-done.1.win_s
  33.6 0.0 copy-start
  33.6 0.0 collective-permute-done.3.wback_s
  33.6 0.5 copy-done.2
  34.1 0.2 copy-done.1
  34.3 0.7 copy-done
  35.0 78.7 %ffn.1 = (f32[1024,512]{1,0:T(8,128)}, f32[1024,512]{1,0:T(8,128)}, f32[1024,512]{1,0:T(8,128)}, f32[2,128,8,128]{3,2,1,0:T(8,128)}, f32[2,8,512]{2,1,0:T(8,128)...) custom-call(f32[256,512]{1,0:T(8,128)} %copy-done.1, f32[256,512]{1,0:T(8,128)} %wout_o.1, ...), custom_call_target="tpu_custom_call" | custom-call | tf_op jit(solution)/shard_map/ffn/pallas_call | solution.py:870
  113.8 108.7 %attn_bwd.1 = (f32[1024,512]{1,0:T(8,128)}, f32[768,512]{1,0:T(8,128)}, f32[512,768]{1,0:T(8,128)}, f32[256,512]{1,0:T(8,128)}, f32[3,512,128]{2,1,0:T(8,128)}, ...) custom-call(f32[1,512]{1,0:T(1,128)} %bitcast.14, f32[1,512]{1,0:T(1,128)} %bitcast.16, s32[2,1024]{1,0:T(2,128)} %segs.3, ...), custom_call_target="tpu_custom_call" | custom-call | tf_op jit(solution)/shard_map/attn_bwd/pallas_call | solution.py:903
  222.4 8.3 %place.1 = (f32[1024,512]{1,0:T(8,128)}, f32[1024,512]{1,0:T(8,128)}, f32[1024,512]{1,0:T(8,128)}, f32[512,1024]{1,0:T(8,128)}, f32[256,512]{1,0:T(8,128)}, /*in...) custom-call(f32[1024,512]{1,0:T(8,128)} %get-tuple-element.55.output, ...), custom_call_target="tpu_custom_call" | custom-call | tf_op jit(solution)/shard_map/place/pallas_call | solution.py:958
Async XLA Ops:
  0.6 32.9 %collective-permute-start.1 = (f32[512,1024]{1,0:T(8,128)}, f32[512,1024]{1,0:T(8,128)S(1)}, u32[]{:S(2)}, u32[]{:S(2)}) collective-permute-start(f32[512,1024]{1,0:T(8,128)} %win_o.1), channel_id=1, source_target_pairs={{0,1},{1,0},{2,3},{3,2},{4,5},{5,4},{6,7},{7,6},{8,9},{9,8},{10,11... | collective-permute-start | bytes 6291464 | tf_op jit(solution)/shard_map/ppermute | solution.py:982
  1.2 32.4 %collective-permute-start.3 = (f32[1024,512]{1,0:T(8,128)}, f32[1024,512]{1,0:T(8,128)}, u32[]{:S(2)}, u32[]{:S(2)}) collective-permute-start(f32[1024,512]{1,0:T(8,128)} %wback_o.1), channel_id=1, source_target_pairs={{0,1},{1,0},{2,3},{3,2},{4,5},{5,4},{6,7},{7,6},{8,9},{9,8},{10,11... | collective-permute-start | bytes 6291464 | tf_op jit(solution)/shard_map/ppermute | solution.py:982
  1.2 32.3 %collective-permute-start.2 = (f32[1024]{0:T(1024)}, f32[1024]{0:T(1024)S(1)}, u32[]{:S(2)}, u32[]{:S(2)}) collective-permute-start(f32[1024]{0:T(1024)} %param.24), channel_id=1, source_target_pairs={{0,1},{1,0},{2,3},{3,2},{4,5},{5,4},{6,7},{7,6},{8,9},{9,8},{10,11... | collective-permute-start | bytes 12296 | tf_op jit(solution)/shard_map/ppermute | solution.py:982
  1.7 31.9 %collective-permute-start = (f32[256,512]{1,0:T(8,128)}, f32[256,512]{1,0:T(8,128)S(1)}, u32[]{:S(2)}, u32[]{:S(2)}) collective-permute-start(f32[256,512]{1,0:T(8,128)} %wout_o.1), channel_id=1, source_target_pairs={{0,1},{1,0},{2,3},{3,2},{4,5},{5,4},{6,7},{7,6},{8,9},{9,8},{10,11... | collective-permute-start | bytes 1572872 | tf_op jit(solution)/shard_map/ppermute | solution.py:982
  33.5 0.6 copy-start.2
  33.5 0.8 copy-start.1
  33.6 1.5 copy-start
